TPU v7x, 256 devices: a whole 4x4x8 slice. The times are simulated.
256 devices in a mesh: member: 16 (over y, x), band: 16 (over z, core).
Axes of the slice: x: 4, y: 4, z: 8, core: 2. Of those that a mesh axis runs over, the one named last changes fastest.
Arguments:
- ensemble: bfloat16 [16, 64, 80, 1440], P('member', 'band'), may hold values from -6 to 6
- mix_weight: bfloat16 [3, 80, 80], replicated, may hold values from -0.625 to 0.625
- analysis: bfloat16 [64, 80, 1440], P('band', 'member'), may hold values from -4 to 4
- station_weight: bfloat16 [256, 32, 4, 128], P('band'), may hold values from -0.25 to 0.25
- station_obs: bfloat16 [256, 32, 80], P('band'), may hold values from -4 to 4
- block_band: int32 [256, 1], replicated, may hold values from 0 to 15; in each aligned block of 16 rows (0 to 15, 16 to 31, ...) at most 2 rows name the same one
- block_start: int32 [256], replicated, may hold values from 0 to 1312
Outputs:
- grid_score: float32 [64, 80, 1440], P('band', 'member')
- station_score: float32 [256, 32, 80], P('band')
- state_grad: bfloat16 [16, 64, 80, 1440], P('member', 'band')
Inputs may be any that keep to these rules, and one draw needn't show every extreme that they name: `block_band`: blocks 16 b to 16 (b + 1) - 1 are stored with band b. Within each such group no band index appears more than 2 times, and some band index appears exactly 2 times.
All inputs are finite; a program needn't handle non-finite values.
Results may differ from a plain program's by a relative error of at most 0.012.
Values may be sent and summed in bfloat16 or wider, within the bound.
A program may use at most 128 MiB of HBM per device.

v0:
```python
import math

import jax
import jax.numpy as jnp
from jax import lax
from jax.sharding import PartitionSpec as P

CAP = 2


DIFFUSION = 4.0


def with_halo(block, sides, width):
    for axis, dim in sides:
        count = lax.axis_size(axis)
        forward = [(i, i + 1) for i in range(count - 1)]
        backward = [(target, source) for source, target in forward]
        low = lax.ppermute(
            lax.slice_in_dim(block, block.shape[dim] - width, None, axis=dim), axis, forward
        )
        high = lax.ppermute(lax.slice_in_dim(block, 0, width, axis=dim), axis, backward)
        block = jnp.concatenate([low, block, high], axis=dim)
    return block


def kernel_value(spread):
    return jnp.sqrt(spread * spread + 1.0) - 1.0


def kernel_slope(spread):
    return spread / jnp.sqrt(spread * spread + 1.0)


def metric_rows(global_rows, total_rows):
    latitude = math.pi * ((global_rows.astype(jnp.float32) + 0.5) / total_rows - 0.5)
    cosine = jnp.cos(latitude)
    return 1.0 / (cosine * cosine + 0.1)


def inverse_table(points):
    centre = 1.0 + 2.0 * DIFFUSION
    decay_root = (centre - math.sqrt(centre * centre - 4.0 * DIFFUSION * DIFFUSION)) / (
        2.0 * DIFFUSION
    )
    log_root = math.log(decay_root)
    factor = 1.0 / (DIFFUSION * (1.0 / decay_root - decay_root) * (1.0 - decay_root**points))
    column = lax.broadcasted_iota(jnp.int32, (points, points), 0)
    across = lax.broadcasted_iota(jnp.int32, (points, points), 1)
    offset = jnp.abs(column - across)
    nearest = jnp.minimum(offset, points - offset).astype(jnp.float32)
    values = (jnp.exp(nearest * log_root) + jnp.exp((points - nearest) * log_root)) * factor
    return values.astype(jnp.bfloat16)


def stencil_layer(extended, global_rows, weight, total_rows):
    middle = extended[1:-1].astype(jnp.float32)
    north = extended[2:].astype(jnp.float32)
    south = extended[:-2].astype(jnp.float32)
    metric = metric_rows(global_rows, total_rows)[:, None, None]
    eastward = jnp.roll(middle, -1, axis=2)
    westward = jnp.roll(middle, 1, axis=2)
    laplace = (eastward + westward - 2.0 * middle) * metric + (north + south - 2.0 * middle)
    scaled = (laplace / (2.0 + 2.0 * metric)).astype(jnp.bfloat16)
    mixed = jnp.einsum("fg,rgl->rfl", weight, scaled, preferred_element_type=jnp.float32)
    return (middle + jnp.tanh(mixed)).astype(jnp.bfloat16)


def shards(ensemble, mix_weight, analysis, station_weight, station_obs, block_band, block_start):
    band_count = lax.axis_size("band")
    band_pos = lax.axis_index("band")
    members = lax.axis_size("member")
    member_pos = lax.axis_index("member")
    rows_dev = ensemble.shape[1]
    points = ensemble.shape[3]
    total_rows = rows_dev * band_count
    layers = mix_weight.shape[0]
    current = ensemble[0]
    for layer_pos in range(layers):
        extended = with_halo(current, (("band", 0),), 1)
        global_rows = band_pos * rows_dev + jnp.arange(rows_dev, dtype=jnp.int32)
        current = stencil_layer(extended, global_rows, mix_weight[layer_pos], total_rows)
    inverse = inverse_table(points)
    diffused = jnp.dot(current.reshape(-1, points), inverse, preferred_element_type=jnp.float32)
    diffused = diffused.reshape(current.shape).astype(jnp.bfloat16)
    own_values = diffused.astype(jnp.float32)
    pair_scale = 1.0 / (2.0 * members * (members - 1))
    truth_field = lax.all_gather(analysis, "member", axis=1, tiled=True).astype(jnp.float32)
    zero_start = jnp.zeros_like(own_values)

    def member_step(partial_value, other_member):
        spread = own_values - other_member.astype(jnp.float32)
        return (
            (partial_value[0] + kernel_value(spread), partial_value[1] + kernel_slope(spread)),
            None,
        )

    result, _ = lax.scan(
        member_step,
        (zero_start, zero_start),
        lax.all_gather(diffused[None], "member", axis=0, tiled=True),
    )
    pair_value, pair_slope = result
    error_field = own_values - truth_field
    member_term = kernel_value(error_field) / members - pair_value * pair_scale
    grid_score = lax.psum_scatter(
        member_term.astype(jnp.bfloat16), "member", scatter_dimension=1, tiled=True
    ).astype(jnp.float32)
    grid_grad = kernel_slope(error_field) - pair_slope / (members - 1)
    blocks = station_weight.shape[0]
    stations = station_weight.shape[1]
    window = station_weight.shape[3]
    fields = diffused.shape[1]
    slot_count = band_count * CAP
    band_table = block_band[:, 0].reshape(band_count, blocks)
    start_table = block_start.reshape(band_count, blocks)
    block_order = jnp.arange(blocks, dtype=jnp.int32)
    earlier = (band_table[:, :, None] == band_table[:, None, :]) & (
        block_order[None, :, None] > block_order[None, None, :]
    )
    rank_table = jnp.sum(earlier.astype(jnp.int32), axis=2)
    home_table = jnp.broadcast_to(
        jnp.arange(band_count, dtype=jnp.int32)[:, None], (band_count, blocks)
    )
    slot_start = (
        jnp.zeros((band_count, band_count, CAP), jnp.int32)
        .at[home_table, band_table, rank_table]
        .set(start_table)
    )
    my_start = lax.dynamic_index_in_dim(slot_start, band_pos, 1, keepdims=False).reshape(slot_count)
    my_band = lax.dynamic_index_in_dim(band_table, band_pos, 0, keepdims=False)
    my_rank = lax.dynamic_index_in_dim(rank_table, band_pos, 0, keepdims=False)
    outgoing = (
        jnp.zeros((band_count, CAP) + station_weight.shape[1:], jnp.bfloat16)
        .at[my_band, my_rank]
        .set(station_weight)
    )
    incoming = lax.all_to_all(outgoing, "band", split_axis=0, concat_axis=0, tiled=True).reshape(
        (slot_count,) + station_weight.shape[1:]
    )
    windows = jax.vmap(
        lambda offset_lon: lax.dynamic_slice_in_dim(diffused, offset_lon, window, 2)
    )(my_start)
    estimate = jnp.einsum("qsrw,qrfw->qsf", incoming, windows, preferred_element_type=jnp.float32)
    returned = lax.all_to_all(
        estimate.reshape(band_count, CAP, stations, fields).astype(jnp.bfloat16),
        "band",
        split_axis=0,
        concat_axis=0,
        tiled=True,
    ).astype(jnp.float32)
    own_blocks = returned[my_band, my_rank]
    ensemble_est = lax.all_gather(
        own_blocks[None].astype(jnp.bfloat16), "member", axis=0, tiled=True
    ).astype(jnp.float32)

    def station_step(partial_value, other_member):
        spread = ensemble_est - other_member[None]
        return (
            (partial_value[0] + kernel_value(spread), partial_value[1] + kernel_slope(spread)),
            None,
        )

    zero_est = jnp.zeros_like(ensemble_est)
    (station_value, station_pull), _ = lax.scan(station_step, (zero_est, zero_est), ensemble_est)
    station_miss = ensemble_est - station_obs.astype(jnp.float32)[None]
    station_score = jnp.sum(
        kernel_value(station_miss) / members - station_value * pair_scale, axis=0
    )
    station_slopes = kernel_slope(station_miss) - station_pull / (members - 1)
    own_slope = lax.dynamic_index_in_dim(station_slopes, member_pos, 0, keepdims=False).astype(
        jnp.bfloat16
    )
    slope_out = (
        jnp.zeros((band_count, CAP, stations, fields), jnp.bfloat16)
        .at[my_band, my_rank]
        .set(own_slope)
    )
    slope_in = lax.all_to_all(slope_out, "band", split_axis=0, concat_axis=0, tiled=True).reshape(
        slot_count, stations, fields
    )
    spread_back = jnp.einsum(
        "qsrw,qsf->qrfw", incoming, slope_in, preferred_element_type=jnp.float32
    )

    def place_slot(slot_pos, running):
        first_lon = lax.dynamic_index_in_dim(my_start, slot_pos, 0, keepdims=False)
        piece = lax.dynamic_index_in_dim(spread_back, slot_pos, 0, keepdims=False)
        existing = lax.dynamic_slice_in_dim(running, first_lon, window, 2)
        return lax.dynamic_update_slice_in_dim(running, existing + piece, first_lon, 2)

    station_grad = lax.fori_loop(0, slot_count, place_slot, jnp.zeros(diffused.shape, jnp.float32))
    total_grad = (grid_grad + station_grad).astype(jnp.bfloat16)
    state_grad = lax.dot_general(
        total_grad.reshape(-1, points),
        inverse,
        (((1,), (1,)), ((), ())),
        preferred_element_type=jnp.float32,
    )
    state_grad = state_grad.reshape(diffused.shape).astype(jnp.bfloat16)[None]
    return (grid_score, station_score, state_grad)


def solution(mesh):
    return jax.shard_map(
        shards,
        mesh=mesh,
        in_specs=(
            P("member", "band", None, None),
            P(),
            P("band", "member", None),
            P("band", None, None, None),
            P("band", None, None),
            P(),
            P(),
        ),
        out_specs=(
            P("band", "member", None),
            P("band", None, None),
            P("member", "band", None, None),
        ),
        check_vma=False,
    )
```

profile of v0, /device:TPU:1, one launch (start us, length us, event | category | flops | bytes accessed | tf_op | source)
XLA Modules:
  0.0 786.0 jit_solution(7899435466700482843)
XLA Ops:
  23.7 9.7 %all-to-all-start = ((bf16[16,2,32,4,128]{4,2,3,1,0:T(8,128)(2,1)}), bf16[16,2,32,4,128]{4,2,3,1,0:T(8,128)(2,1)}, u32[]{:S(2)}, u32[]{:S(2)}) async-start(bf16[16,2,32,4,128]{4,2,3,1,0:T(8,128)(2,1)} %scatter_fusion), calls=%async_computation | async-start | bytes 2097152 | tf_op jit(solution)/shard_map/all_to_all | solution.py:138
  36.5 15.4 %scatter_fusion.1 = s32[16,16,2]{1,0,2:T(8,128)S(1)} fusion(s32[16,16,2]{1,0,2:T(8,128)S(1)} %broadcast_in_dim.16, s32[256]{0:T(256)S(1)} %reshape.243, s32[256]{0:T(256)S(1)} %copy-done.6), kind=kCustom, calls=%fused_computation.3 | custom fusion | bytes 6144 | tf_op jit(solution)/shard_map/scatter | solution.py:128
  79.0 9.8 %fusion.133 = (f32[4,80,1440]{2,1,0:T(8,128)}, bf16[4,80,1440]{2,1,0:T(8,128)(2,1)S(1)}) fusion(f32[4,80,1439]{2,1,0:T(8,128)} %get-tuple-element.285, f32[4,80,1]{2,1,0:T(8,128)S(1)} %get-tuple-element.287, f32[4,80,1]{2,1,0:T(8,128)S(1)} %get-tuple-element.286, f32[4,80,1439]{2,1,0:T(8,128)} %get-tuple-element.284, bf16[4,80,1440]{2,1,0:T(8,128)(2,1)S(1)} %fusion.21, ...), kind=kOutput, calls=%fused_computation.174 | convolution fusion | flops 1435161600 | bytes 9255424 | tf_op jit(solution)/shard_map/dot_general | solution.py:84
  90.5 5.9 gather_fusion
  99.6 19.9 %all_to_all.15 = bf16[16,2,32,80]{3,2,1,0:T(8,128)(2,1)S(1)} all-to-all(bf16[16,2,32,80]{3,2,1,0:T(8,128)(2,1)S(1)} %bitcast.138), channel_id=1, replica_groups=mesh['member'=16,'band'=16] {'band'}, dimensions={0} | all-to-all | bytes 327680 | tf_op jit(solution)/shard_map/all_to_all | solution.py:145
  121.7 45.2 %all-gather.7.cloned.1.call-done = bf16[256,32,80]{2,1,0:T(8,128)(2,1)} async-done(((bf16[16,32,80]{2,1,0:T(8,128)(2,1)}), bf16[256,32,80]{2,1,0:T(8,128)(2,1)}) %all-gather.7.cloned.1.call-update) | async-done | bytes 1310736 | tf_op jit(solution)/shard_map/all_gather | solution.py:153
  170.9 180.6 %while.45 = (s32[]{:T(128)}, f32[16,16,32,80]{3,2,1,0:T(8,128)}, f32[16,16,32,80]{3,2,1,0:T(8,128)}, f32[16,16,32,80]{3,2,1,0:T(8,128)}, s32[]{:T(128)}, /*index=5*/s32[]{:T(128)}) while((s32[]{:T(128)}, f32[16,16,32,80]{3,2,1,0:T(8,128)}, f32[16,16,32,80]{3,2,1,0:T(8,128)}, f32[16,16,32,80]{3,2,1,0:T(8,128)}, s32[]{:T(128)}, ...), condition=%wide.region_7.8_spmd.clone, body=%wide.region_6.7_spmd.clone.sunk | while | flops 5898243 | bytes 13598811 | solution.py:165
  172.0 7.8 select_add_fusion.7
  180.8 11.4 %select_add_fusion.7 = (f32[16,16,32,80]{3,2,1,0:T(8,128)}, f32[16,16,32,80]{3,2,1,0:T(8,128)}) fusion(f32[16,16,32,80]{3,2,1,0:T(8,128)} %get-tuple-element.421, f32[16,16,32,80]{3,2,1,0:T(8,128)} %get-tuple-element.428, f32[16,32,80]{2,1,0:T(8,128)S(1)} %dynamic-slice_bitcast_fusion.2, pred[]{:T(512)S(6)} %compare.40, ...), kind=kLoop, calls=%fused_computation.10.clone.1 | loop fusion | flops 5898240 | bytes 13271041 | tf_op jit(solution)/shard_map/while/body/eval_jaxpr/add | solution.py:160
  193.2 10.5 %select_add_fusion.7 = (f32[16,16,32,80]{3,2,1,0:T(8,128)}, f32[16,16,32,80]{3,2,1,0:T(8,128)}) fusion(f32[16,16,32,80]{3,2,1,0:T(8,128)} %get-tuple-element.421, f32[16,16,32,80]{3,2,1,0:T(8,128)} %get-tuple-element.428, f32[16,32,80]{2,1,0:T(8,128)S(1)} %dynamic-slice_bitcast_fusion.2, pred[]{:T(512)S(6)} %compare.40, ...), kind=kLoop, calls=%fused_computation.10.clone.1 | loop fusion | flops 5898240 | bytes 13271041 | tf_op jit(solution)/shard_map/while/body/eval_jaxpr/add | solution.py:160
  204.7 10.4 %select_add_fusion.7 = (f32[16,16,32,80]{3,2,1,0:T(8,128)}, f32[16,16,32,80]{3,2,1,0:T(8,128)}) fusion(f32[16,16,32,80]{3,2,1,0:T(8,128)} %get-tuple-element.421, f32[16,16,32,80]{3,2,1,0:T(8,128)} %get-tuple-element.428, f32[16,32,80]{2,1,0:T(8,128)S(1)} %dynamic-slice_bitcast_fusion.2, pred[]{:T(512)S(6)} %compare.40, ...), kind=kLoop, calls=%fused_computation.10.clone.1 | loop fusion | flops 5898240 | bytes 13271041 | tf_op jit(solution)/shard_map/while/body/eval_jaxpr/add | solution.py:160
  216.2 10.5 %select_add_fusion.7 = (f32[16,16,32,80]{3,2,1,0:T(8,128)}, f32[16,16,32,80]{3,2,1,0:T(8,128)}) fusion(f32[16,16,32,80]{3,2,1,0:T(8,128)} %get-tuple-element.421, f32[16,16,32,80]{3,2,1,0:T(8,128)} %get-tuple-element.428, f32[16,32,80]{2,1,0:T(8,128)S(1)} %dynamic-slice_bitcast_fusion.2, pred[]{:T(512)S(6)} %compare.40, ...), kind=kLoop, calls=%fused_computation.10.clone.1 | loop fusion | flops 5898240 | bytes 13271041 | tf_op jit(solution)/shard_map/while/body/eval_jaxpr/add | solution.py:160
  227.6 10.7 %select_add_fusion.7 = (f32[16,16,32,80]{3,2,1,0:T(8,128)}, f32[16,16,32,80]{3,2,1,0:T(8,128)}) fusion(f32[16,16,32,80]{3,2,1,0:T(8,128)} %get-tuple-element.421, f32[16,16,32,80]{3,2,1,0:T(8,128)} %get-tuple-element.428, f32[16,32,80]{2,1,0:T(8,128)S(1)} %dynamic-slice_bitcast_fusion.2, pred[]{:T(512)S(6)} %compare.40, ...), kind=kLoop, calls=%fused_computation.10.clone.1 | loop fusion | flops 5898240 | bytes 13271041 | tf_op jit(solution)/shard_map/while/body/eval_jaxpr/add | solution.py:160
  239.3 10.6 %select_add_fusion.7 = (f32[16,16,32,80]{3,2,1,0:T(8,128)}, f32[16,16,32,80]{3,2,1,0:T(8,128)}) fusion(f32[16,16,32,80]{3,2,1,0:T(8,128)} %get-tuple-element.421, f32[16,16,32,80]{3,2,1,0:T(8,128)} %get-tuple-element.428, f32[16,32,80]{2,1,0:T(8,128)S(1)} %dynamic-slice_bitcast_fusion.2, pred[]{:T(512)S(6)} %compare.40, ...), kind=kLoop, calls=%fused_computation.10.clone.1 | loop fusion | flops 5898240 | bytes 13271041 | tf_op jit(solution)/shard_map/while/body/eval_jaxpr/add | solution.py:160
  250.9 10.5 %select_add_fusion.7 = (f32[16,16,32,80]{3,2,1,0:T(8,128)}, f32[16,16,32,80]{3,2,1,0:T(8,128)}) fusion(f32[16,16,32,80]{3,2,1,0:T(8,128)} %get-tuple-element.421, f32[16,16,32,80]{3,2,1,0:T(8,128)} %get-tuple-element.428, f32[16,32,80]{2,1,0:T(8,128)S(1)} %dynamic-slice_bitcast_fusion.2, pred[]{:T(512)S(6)} %compare.40, ...), kind=kLoop, calls=%fused_computation.10.clone.1 | loop fusion | flops 5898240 | bytes 13271041 | tf_op jit(solution)/shard_map/while/body/eval_jaxpr/add | solution.py:160
  262.4 10.3 %select_add_fusion.7 = (f32[16,16,32,80]{3,2,1,0:T(8,128)}, f32[16,16,32,80]{3,2,1,0:T(8,128)}) fusion(f32[16,16,32,80]{3,2,1,0:T(8,128)} %get-tuple-element.421, f32[16,16,32,80]{3,2,1,0:T(8,128)} %get-tuple-element.428, f32[16,32,80]{2,1,0:T(8,128)S(1)} %dynamic-slice_bitcast_fusion.2, pred[]{:T(512)S(6)} %compare.40, ...), kind=kLoop, calls=%fused_computation.10.clone.1 | loop fusion | flops 5898240 | bytes 13271041 | tf_op jit(solution)/shard_map/while/body/eval_jaxpr/add | solution.py:160
  273.6 10.3 %select_add_fusion.7 = (f32[16,16,32,80]{3,2,1,0:T(8,128)}, f32[16,16,32,80]{3,2,1,0:T(8,128)}) fusion(f32[16,16,32,80]{3,2,1,0:T(8,128)} %get-tuple-element.421, f32[16,16,32,80]{3,2,1,0:T(8,128)} %get-tuple-element.428, f32[16,32,80]{2,1,0:T(8,128)S(1)} %dynamic-slice_bitcast_fusion.2, pred[]{:T(512)S(6)} %compare.40, ...), kind=kLoop, calls=%fused_computation.10.clone.1 | loop fusion | flops 5898240 | bytes 13271041 | tf_op jit(solution)/shard_map/while/body/eval_jaxpr/add | solution.py:160
  284.9 10.3 %select_add_fusion.7 = (f32[16,16,32,80]{3,2,1,0:T(8,128)}, f32[16,16,32,80]{3,2,1,0:T(8,128)}) fusion(f32[16,16,32,80]{3,2,1,0:T(8,128)} %get-tuple-element.421, f32[16,16,32,80]{3,2,1,0:T(8,128)} %get-tuple-element.428, f32[16,32,80]{2,1,0:T(8,128)S(1)} %dynamic-slice_bitcast_fusion.2, pred[]{:T(512)S(6)} %compare.40, ...), kind=kLoop, calls=%fused_computation.10.clone.1 | loop fusion | flops 5898240 | bytes 13271041 | tf_op jit(solution)/shard_map/while/body/eval_jaxpr/add | solution.py:160
  296.2 10.3 %select_add_fusion.7 = (f32[16,16,32,80]{3,2,1,0:T(8,128)}, f32[16,16,32,80]{3,2,1,0:T(8,128)}) fusion(f32[16,16,32,80]{3,2,1,0:T(8,128)} %get-tuple-element.421, f32[16,16,32,80]{3,2,1,0:T(8,128)} %get-tuple-element.428, f32[16,32,80]{2,1,0:T(8,128)S(1)} %dynamic-slice_bitcast_fusion.2, pred[]{:T(512)S(6)} %compare.40, ...), kind=kLoop, calls=%fused_computation.10.clone.1 | loop fusion | flops 5898240 | bytes 13271041 | tf_op jit(solution)/shard_map/while/body/eval_jaxpr/add | solution.py:160
  307.4 10.3 %select_add_fusion.7 = (f32[16,16,32,80]{3,2,1,0:T(8,128)}, f32[16,16,32,80]{3,2,1,0:T(8,128)}) fusion(f32[16,16,32,80]{3,2,1,0:T(8,128)} %get-tuple-element.421, f32[16,16,32,80]{3,2,1,0:T(8,128)} %get-tuple-element.428, f32[16,32,80]{2,1,0:T(8,128)S(1)} %dynamic-slice_bitcast_fusion.2, pred[]{:T(512)S(6)} %compare.40, ...), kind=kLoop, calls=%fused_computation.10.clone.1 | loop fusion | flops 5898240 | bytes 13271041 | tf_op jit(solution)/shard_map/while/body/eval_jaxpr/add | solution.py:160
  318.7 10.3 %select_add_fusion.7 = (f32[16,16,32,80]{3,2,1,0:T(8,128)}, f32[16,16,32,80]{3,2,1,0:T(8,128)}) fusion(f32[16,16,32,80]{3,2,1,0:T(8,128)} %get-tuple-element.421, f32[16,16,32,80]{3,2,1,0:T(8,128)} %get-tuple-element.428, f32[16,32,80]{2,1,0:T(8,128)S(1)} %dynamic-slice_bitcast_fusion.2, pred[]{:T(512)S(6)} %compare.40, ...), kind=kLoop, calls=%fused_computation.10.clone.1 | loop fusion | flops 5898240 | bytes 13271041 | tf_op jit(solution)/shard_map/while/body/eval_jaxpr/add | solution.py:160
  330.0 10.3 %select_add_fusion.7 = (f32[16,16,32,80]{3,2,1,0:T(8,128)}, f32[16,16,32,80]{3,2,1,0:T(8,128)}) fusion(f32[16,16,32,80]{3,2,1,0:T(8,128)} %get-tuple-element.421, f32[16,16,32,80]{3,2,1,0:T(8,128)} %get-tuple-element.428, f32[16,32,80]{2,1,0:T(8,128)S(1)} %dynamic-slice_bitcast_fusion.2, pred[]{:T(512)S(6)} %compare.40, ...), kind=kLoop, calls=%fused_computation.10.clone.1 | loop fusion | flops 5898240 | bytes 13271041 | tf_op jit(solution)/shard_map/while/body/eval_jaxpr/add | solution.py:160
  341.2 10.3 %select_add_fusion.7 = (f32[16,16,32,80]{3,2,1,0:T(8,128)}, f32[16,16,32,80]{3,2,1,0:T(8,128)}) fusion(f32[16,16,32,80]{3,2,1,0:T(8,128)} %get-tuple-element.421, f32[16,16,32,80]{3,2,1,0:T(8,128)} %get-tuple-element.428, f32[16,32,80]{2,1,0:T(8,128)S(1)} %dynamic-slice_bitcast_fusion.2, pred[]{:T(512)S(6)} %compare.40, ...), kind=kLoop, calls=%fused_computation.10.clone.1 | loop fusion | flops 5898240 | bytes 13271041 | tf_op jit(solution)/shard_map/while/body/eval_jaxpr/add | solution.py:160
  351.5 6.9 broadcast_subtract_fusion
  362.5 8.6 %all-to-all-start.2 = ((bf16[16,2,32,80]{3,2,1,0:T(8,128)(2,1)}), bf16[16,2,32,80]{3,2,1,0:T(8,128)(2,1)S(1)}, u32[]{:S(2)}, u32[]{:S(2)}) async-start(bf16[16,2,32,80]{3,2,1,0:T(8,128)(2,1)} %scatter_fusion.2), calls=%async_computation.2 | async-start | bytes 524288 | tf_op jit(solution)/shard_map/all_to_all | solution.py:179
  372.6 22.2 %all_gather.9 = bf16[4,80,1440]{2,0,1:T(4,128)(2,1)} all-gather(bf16[4,5,1440]{2,0,1:T(4,128)(2,1)S(1)} %copy-done.7), channel_id=1, replica_groups=mesh['member'=16,'band'=16] {'member'}, dimensions={1}, use_global_device_ids=true | all-gather | bytes 979200 | tf_op jit(solution)/shard_map/all_gather | solution.py:88
  400.7 183.2 %while.43 = (s32[]{:T(128)}, f32[4,80,1440]{2,1,0:T(8,128)}, s32[32]{0:T(128)S(1)}, f32[32,4,80,128]{3,2,1,0:T(8,128)}, s32[]{:T(128)}, /*index=5*/s32[]{:T(128)}, s32[]{:T(128)}) while((s32[]{:T(128)}, f32[4,80,1440]{2,1,0:T(8,128)}, s32[32]{0:T(128)S(1)}, f32[32,4,80,128]{3,2,1,0:T(8,128)}, s32[]{:T(128)}, /*index=5*/s32[]{:T(128)}, ...), condition=%wide.region_11.12_spmd, body=%wide.region_10.11_spmd.sunk | while | flops 40965 | bytes 819343 | solution.py:192
  583.9 83.8 %while.44 = (s32[]{:T(128)}, f32[4,80,1440]{2,1,0:T(8,128)S(1)}, f32[4,80,1440]{2,1,0:T(8,128)}, bf16[16,4,80,1440]{3,2,1,0:T(8,128)(2,1)}, f32[4,80,1440]{2,1,0:T(8,128)}, /*index=5*/s32[]{:T(128)}, s32[]{:T(128)}) while((s32[]{:T(128)}, f32[4,80,1440]{2,1,0:T(8,128)S(1)}, f32[4,80,1440]{2,1,0:T(8,128)}, ...), condition=%wide.region_1.2_spmd.clone, body=%wide.region_0.1_spmd.clone.sunk | while | flops 4608003 | bytes 10137699 | solution.py:98
  588.7 5.3 select_add_fusion.6
  620.3 5.3 select_add_fusion.6
  671.8 8.9 %fusion.29 = bf16[1,4,80,1440]{3,2,1,0:T(8,128)(2,1)} fusion(f32[4,80,1440]{2,1,0:T(8,128)} %get-tuple-element.206, f32[4,80,1440]{2,1,0:T(8,128)S(1)} %copy-done, bf16[4,80,1440]{2,1,0:T(8,128)(2,1)S(1)} %copy-done.3, bf16[4,80,1440]{2,0,1:T(4,128)(2,1)} %all_gather.9), kind=kOutput, calls=%fused_computation.44 | convolution fusion | flops 1354982400 | bytes 6451200 | tf_op jit(solution)/shard_map/dot_general | solution.py:194
  680.7 97.0 %all-reduce.4.cloned.1.call-done = bf16[4,80,1440]{2,0,1:T(4,128)(2,1)} async-done(((bf16[4,80,1440]{2,0,1:T(4,128)(2,1)}), bf16[4,80,1440]{2,0,1:T(4,128)(2,1)}) %all-reduce.4.cloned.1.call-update) | async-done | bytes 921616
  (218 shorter events, 284.8 us)
Async XLA Ops:
  9.0 43.5 %collective-permute-start.1 = (bf16[1,80,1440]{2,1,0:T(8,128)(2,1)}, bf16[1,80,1440]{2,1,0:T(8,128)(2,1)}, u32[]{:S(2)}, u32[]{:S(2)}) collective-permute-start(bf16[1,80,1440]{2,1,0:T(8,128)(2,1)} %get-tuple-element.295), channel_id=1, source_target_pairs={{0,1},{1,2},{2,3},{3,4},{4,5},{5,6},{6,7},{7,8},{8,9},{9,10},{10,1... | collective-permute-start | bytes 691208 | tf_op jit(solution)/shard_map/ppermute | solution.py:19
  13.9 38.6 %collective-permute-start = (bf16[1,80,1440]{2,1,0:T(8,128)(2,1)S(1)}, bf16[1,80,1440]{2,1,0:T(8,128)(2,1)}, u32[]{:S(2)}, u32[]{:S(2)}) collective-permute-start(bf16[1,80,1440]{2,1,0:T(8,128)(2,1)S(1)} %get-tuple-element.294), channel_id=1, source_target_pairs={{1,0},{2,1},{3,2},{4,3},{5,4},{6,5},{7,6},{8,7},{9,8},{10,9},{11,1... | collective-permute-start | bytes 691208 | tf_op jit(solution)/shard_map/ppermute | solution.py:22
  20.9 12.5 %copy-start.4 = (bf16[1,4,80,1440]{3,2,1,0:T(8,128)(2,1)S(1)}, bf16[1,4,80,1440]{3,2,1,0:T(8,128)(2,1)}, u32[]{:S(2)}) copy-start(bf16[1,4,80,1440]{3,2,1,0:T(8,128)(2,1)} %param.13) | copy-start | bytes 2764804
  23.7 72.8 %all-to-all-start = ((bf16[16,2,32,4,128]{4,2,3,1,0:T(8,128)(2,1)}), bf16[16,2,32,4,128]{4,2,3,1,0:T(8,128)(2,1)}, u32[]{:S(2)}, u32[]{:S(2)}) async-start(bf16[16,2,32,4,128]{4,2,3,1,0:T(8,128)(2,1)} %scatter_fusion), calls=%async_computation | async-start | bytes 2097152 | tf_op jit(solution)/shard_map/all_to_all | solution.py:138
  33.3 133.5 %all-gather.7.cloned.1.call-start = ((), (), s32[]{:S(2)}) async-start(), calls=%async_computation.4 | async-start | bytes 2228224 | tf_op jit(solution)/shard_map/all_gather | solution.py:153
  33.6 2.7 copy-start.8
  33.6 2.8 copy-start.6
  36.5 16.0 %copy-start.9 = (bf16[3,80,80]{2,1,0:T(8,128)(2,1)S(1)}, bf16[3,80,80]{2,1,0:T(8,128)(2,1)}, u32[]{:S(2)}) copy-start(bf16[3,80,80]{2,1,0:T(8,128)(2,1)} %param.14) | copy-start | bytes 115204
  56.5 6.7 collective-permute-start.3
  60.1 7.5 collective-permute-start.2
  69.6 7.3 collective-permute-start.5
  71.5 7.5 collective-permute-start.4
  88.8 7.6 copy-start.2
  99.6 22.0 %copy-start.5 = (bf16[16,32,80]{2,1,0:T(8,128)(2,1)S(1)}, bf16[16,32,80]{2,1,0:T(8,128)(2,1)}, u32[]{:S(2)}) copy-start(bf16[16,32,80]{2,1,0:T(8,128)(2,1)} %param.17) | copy-start | bytes 245764
  120.8 463.1 %all-gather.5.cloned.1.call-start = ((), (), s32[]{:S(2)}) async-start(), calls=%async_computation.3 | async-start | bytes 16711680 | tf_op jit(solution)/shard_map/all_gather | solution.py:101
  170.9 180.6 %copy-start.1 = (bf16[256,32,80]{2,1,0:T(8,128)(2,1)S(1)}, bf16[256,32,80]{2,1,0:T(8,128)(2,1)}, u32[]{:S(2)}) copy-start(bf16[256,32,80]{2,1,0:T(8,128)(2,1)} %all-gather.7.cloned.1.call-done) | copy-start | bytes 3932164
  358.4 12.8 %copy-start.10 = (u32[256]{0:T(256)S(1)}, u32[256]{0:T(256)}, u32[]{:S(2)}) copy-start(u32[256]{0:T(256)} %constant.267) | copy-start | bytes 3076
  358.4 14.2 %copy-start.7 = (bf16[4,5,1440]{2,0,1:T(4,128)(2,1)S(1)}, bf16[4,5,1440]{2,0,1:T(4,128)(2,1)}, u32[]{:S(2)}) copy-start(bf16[4,5,1440]{2,0,1:T(4,128)(2,1)} %param.15) | copy-start | bytes 172804
  362.5 32.3 %all-to-all-start.2 = ((bf16[16,2,32,80]{3,2,1,0:T(8,128)(2,1)}), bf16[16,2,32,80]{3,2,1,0:T(8,128)(2,1)S(1)}, u32[]{:S(2)}, u32[]{:S(2)}) async-start(bf16[16,2,32,80]{3,2,1,0:T(8,128)(2,1)} %scatter_fusion.2), calls=%async_computation.2 | async-start | bytes 524288 | tf_op jit(solution)/shard_map/all_to_all | solution.py:179
  371.1 406.7 %all-reduce.4.cloned.1.call-start = ((), (), s32[]{:S(2)}) async-start(), calls=%async_computation.5 | async-start | bytes 1966080
  583.9 83.8 %copy-start.3 = (bf16[4,80,1440]{2,1,0:T(8,128)(2,1)S(1)}, bf16[4,80,1440]{2,1,0:T(8,128)(2,1)}, u32[]{:S(2)}) copy-start(bf16[4,80,1440]{2,1,0:T(8,128)(2,1)} %copy-done.2) | copy-start | bytes 2764804
  670.0 1.7 copy-start
Sparse Core Ops, SparseCore 0:
  121.0 45.8 all-gather.6
  169.8 111.1 all-gather.4
  671.9 105.8 all-reduce.3
where the time goes:
time: 795 us; the launch traced here: 786 us
  other arithmetic  304 us (38%)
  waiting for transfers between devices  150 us (19%)
  local copies, waits for them, and re-layouts  145 us (18%)
  loops' own time  61.3 us (8%)
  blocking collectives  42.2 us (5%)
  starting transfers between devices  35.9 us (5%)
  matrix products  31.7 us (4%)
  between operations  15 us (2%)
    add x16, other arithmetic, station_step(): partial_value[1] + kernel_slope(spread)  165 us
    unnamed x4, waiting for transfers between devices  97.6 us
    add x16, other arithmetic, member_step(): partial_value[1] + kernel_slope(spread)  83.8 us
    dynamic_update_slice x32, local copies, waits for them, and re-layouts, place_slot(): lax.dynamic_update_slice_in_dim(running, existing + piece, first_lon, 2)  65.1 us
    another operation x1, loops' own time, shards(): lax.fori_loop(0, slot_count, place_slot, jnp.zeros(diffused.shape, jnp.fl...  61.2 us
    all_gather x1, waiting for transfers between devices, shards(): lax.all_gather(own_blocks[None].astype(jnp.bfloat16), 'member', axis=0, t...  45.2 us
    add x32, other arithmetic, place_slot(): existing + piece  37.6 us
    all_gather x1, blocking collectives, shards(): lax.all_gather(analysis, 'member', axis=1, tiled=True).astype(jnp.float32)  22.2 us
  transfers between devices with their start and end apart: 11, of which 5 were waited for; matrix products, arithmetic and copies ran while one was open for 49% of the time, Pallas kernels for 0%

commit v1 on v0

v1 whole, which is shorter than its diff:
```python
import math

import jax
import jax.numpy as jnp
import numpy as np
from jax import lax
from jax.experimental import pallas as pl
from jax.experimental.pallas import tpu as pltpu
from jax.sharding import PartitionSpec as P

CAP = 2
DIFFUSION = 4.0

ROWS = 4
HALO = 3
EXT = ROWS + 2 * HALO
FIELDS = 80
LON = 1440
LANES = 1536
QUARTER = LANES // 4
MSG = LANES + QUARTER
MEMBERS = 16
BANDS = 16
TOTAL_ROWS = 64
LAYERS = 3
SLOTS = BANDS * CAP
STATIONS = 32
POINTS = SLOTS * STATIONS
PAIRS = MEMBERS * (MEMBERS - 1) // 2
MIB = 1 << 20

BF = jnp.bfloat16
F32 = jnp.float32


def inverse_table():
    centre = 1.0 + 2.0 * DIFFUSION
    root = (centre - math.sqrt(centre * centre - 4.0 * DIFFUSION * DIFFUSION)) / (2.0 * DIFFUSION)
    factor = 1.0 / (DIFFUSION * (1.0 / root - root) * (1.0 - root**LON))
    offset = np.abs(np.arange(LON)[:, None] - np.arange(LON)[None, :])
    nearest = np.minimum(offset, LON - offset).astype(np.float64)
    values = (np.exp(nearest * math.log(root)) + np.exp((LON - nearest) * math.log(root))) * factor
    table = np.zeros((LANES, LANES), np.float32)
    table[:LON, :LON] = values
    return table.astype(BF)


def row_factors():
    rows = np.arange(-HALO, TOTAL_ROWS + HALO)
    cosine = np.cos(math.pi * ((rows + 0.5) / TOTAL_ROWS - 0.5))
    metric = 1.0 / (cosine * cosine + 0.1)
    inside = (rows >= 0) & (rows < TOTAL_ROWS)
    return np.stack([metric / (2 + 2 * metric), 1 / (2 + 2 * metric), inside], axis=1).astype(np.float32)


def hot(condition):
    return jnp.where(condition, 1.0, 0.0).astype(BF)


def iota(shape, dim):
    return lax.broadcasted_iota(jnp.int32, shape, dim)


def grid_to_message(transposed):
    shape = (320, 256) if transposed else (256, 320)
    row, col = iota(shape, int(transposed)), iota(shape, 1 - int(transposed))
    group, place = row >> 4, row & 15
    main = hot(col == (place >> 2) * FIELDS + group * 5 + (place & 3))
    fifth = (col == (place & 3) * FIELDS + group * 5 + 4)
    return main, [hot(fifth & ((place >> 2) == q)) for q in range(4)]


def message_to_station(transposed):
    shape = (256, 512) if transposed else (512, 256)
    row, col = iota(shape, int(transposed)), iota(shape, 1 - int(transposed))
    r, member, f = row >> 7, (row >> 3) & 15, row & 7
    same = member == (col >> 4)
    place = col & 15
    main = hot(same & (f < 4) & (place == r * 4 + f))
    return main, [hot(same & (f == 4) & (place == q * 4 + r)) for q in range(4)]


def dot(a, b):
    return jnp.dot(a, b, preferred_element_type=F32)


def dot_t(a, b):
    return lax.dot_general(a, b, (((1,), (1,)), ((), ())), preferred_element_type=F32)


def stencil_row(u, nxt, scaled, weight, row, east_west, north_south, inside):
    tiles = LANES // 128
    lane = iota((FIELDS, 128), 1)

    def tile(at, t):
        return u[at, :, t * 128 : (t + 1) * 128].astype(F32)

    first, last = tile(row, 0), tile(row, tiles - 1)
    wrapped = jnp.where(lane == LON % 128, pltpu.roll(first, LON % 128, 1), last)
    before = pltpu.roll(last, 129 - LON % 128, 1)
    here = first
    for t in range(tiles):
        after = wrapped if t == tiles - 2 else (tile(row, t + 1) if t < tiles - 1 else here)
        east = jnp.where(lane == 127, pltpu.roll(after, 127, 1), pltpu.roll(here, 127, 1))
        moved = pltpu.roll(here, 1, 1)
        west = jnp.where(lane == 0, before, moved)
        sides = tile(row - 1, t) + tile(row + 1, t)
        value = (east + west) * east_west + sides * north_south - here
        scaled[:, t * 128 : (t + 1) * 128] = value.astype(BF)
        before, here = moved, after
    for t in range(0, LANES, 256):
        mixed = dot(weight, scaled[:, t : t + 256])
        fresh = u[row, :, t : t + 256].astype(F32) + jnp.tanh(mixed)
        nxt[row, :, t : t + 256] = (fresh * inside).astype(BF)


def diffuse_to_message(state, inverse_ref, message_ref):
    main, fifth = grid_to_message(False)
    folded = jnp.zeros((256, QUARTER), F32)
    rows = state[HALO : HALO + ROWS].reshape(ROWS * FIELDS, LANES)
    for q in range(4):
        at = slice(q * QUARTER, (q + 1) * QUARTER)
        piece = dot(rows, inverse_ref[:, at]).astype(BF)
        message_ref[:, :, at] = dot(main, piece).astype(BF).reshape(MEMBERS, 16, QUARTER)
        folded += dot(fifth[q], piece)
    message_ref[:, :, LANES:] = folded.astype(BF).reshape(MEMBERS, 16, QUARTER)


def pair_terms(values, truth):
    slopes = [None] * MEMBERS
    total = None
    for i in range(MEMBERS):
        for j in range(i + 1, MEMBERS):
            spread = values[i] - values[j]
            square = spread * spread + 1.0
            inverse = lax.rsqrt(square)
            slope = spread * inverse
            root = square * inverse
            total = root if total is None else total + root
            slopes[i] = slope if slopes[i] is None else slopes[i] + slope
            slopes[j] = -slope if slopes[j] is None else slopes[j] - slope
    error_total = None
    grads = []
    for m in range(MEMBERS):
        error = values[m] - truth
        square = error * error + 1.0
        inverse = lax.rsqrt(square)
        root = square * inverse
        error_total = root if error_total is None else error_total + root
        grads.append(error * inverse - slopes[m] * (1.0 / (MEMBERS - 1)))
    score = (error_total - MEMBERS) * (1.0 / MEMBERS) - (total - PAIRS) * (1.0 / (MEMBERS * (MEMBERS - 1)))
    return score, grads


def send(src, dst, sems, at, device):
    return pltpu.make_async_remote_copy(
        src_ref=src,
        dst_ref=dst,
        send_sem=sems.at[0, at],
        recv_sem=sems.at[1, at],
        device_id=device,
        device_id_type=pl.DeviceIdType.MESH,
    )


def member_at(member, step, sign):
    x = (member + sign * (step & 3)) & 3
    y = ((member >> 2) + sign * (step >> 2)) & 3
    return y * 4 + x


def band_at(band, step, sign):
    return (band + sign * step) & (BANDS - 1)


def exchange(source, target, sems, me, at, axis):
    @pl.loop(1, 16)
    def _(step):
        peer = at(me, step, 1)
        send(source(peer), target(me), sems, step, {axis: peer}).start()


def wait_received(source, target, sems, me, at, axis):
    @pl.loop(1, 16)
    def _(step):
        peer = at(me, step, -1)
        send(source(peer), target(peer), sems, step, {axis: peer}).wait_recv()


def wait_sent(source, target, sems, me, at, axis):
    @pl.loop(1, 16)
    def _(step):
        peer = at(me, step, 1)
        send(source(peer), target(me), sems, step, {axis: peer}).wait_send()


def outgoing_blocks(slot_ref, share_ref, obs_ref, zout):
    lane = iota((1, 128), 1)
    slot_row = jnp.zeros((1, 128), jnp.int32)
    for k in range(16):
        slot_row = jnp.where((lane >> 3) == k, slot_ref[k], slot_row)
    row, col = iota((256, 128), 0), iota((256, 128), 1)
    pick = hot(((row >> 3) == slot_row) & ((row & 7) == (col & 7)))
    zout[:, 0:16, :] = dot(pick, share_ref[...]).astype(BF).reshape(BANDS, 16, 128)
    group = iota((8, 128), 1) >> 5
    for t in range(SLOTS // 4):
        tile = jnp.zeros((8, 128), F32)
        for k in range(16):
            tile = jnp.where(group + 4 * t == slot_ref[k], obs_ref[k], tile)
        for odd in range(2):
            piece = pltpu.roll(tile, 64, 1) if odd else tile
            zout[2 * t + odd, 16:32, :] = jnp.concatenate([piece, jnp.zeros((8, 128), F32)], axis=0).astype(BF)


def spread_out_weights(start_ref, weights, spread_weight):
    lane = iota((STATIONS, 128), 1)

    @pl.loop(0, BANDS)
    def _(home):
        blocks = [weights[r * 4 : r * 4 + 4, home].astype(F32) for r in range(ROWS)]
        for cap in range(CAP):
            start = start_ref[home * CAP + cap]
            shift = start & 127
            at = pl.ds(home * 64 + cap * STATIONS, STATIONS)
            moved = [
                pltpu.roll(block[:, cap * 8 : cap * 8 + 8, :].reshape(STATIONS, 128), shift, 1)
                for block in blocks
            ]
            for t in range(LANES // 128):
                place = lane + t * 128 - start
                inside = (place >= 0) & (place < 128)
                for r in range(ROWS):
                    spread_weight[r, at, t * 128 : (t + 1) * 128] = jnp.where(inside, moved[r], 0.0).astype(BF)


def fold_truth(truth_ref, truth):
    truth[...] = jnp.zeros((16, MSG), F32)
    for r in range(ROWS):
        row = truth_ref[r].astype(F32)
        truth[4 * r : 4 * r + 4, :LON] = row[0:4]
        for q in range(4):
            width = min(QUARTER, LON - q * QUARTER)
            truth[4 * q + r : 4 * q + r + 1, LANES : LANES + width] = row[4:5, q * QUARTER : q * QUARTER + width]


def join_obs(zin, obs):
    lane = iota((8, 128), 1)
    for t in range(POINTS // 128):
        low = zin[2 * t, 16:32, :].astype(F32)[0:8]
        high = zin[2 * t + 1, 16:32, :].astype(F32)[0:8]
        obs[:, t * 128 : (t + 1) * 128] = jnp.where(lane < 64, low, pltpu.roll(high, 64, 1))


def station_part(received, rows, est, slopes, spread_weight, spread, obs, station_out):
    main, fifth = message_to_station(False)
    for q in range(4):
        at = slice(q * QUARTER, (q + 1) * QUARTER)
        rows[:, at] = (
            dot(main, received[:, :, at].reshape(256, QUARTER))
            + dot(fifth[q], received[:, :, LANES:].reshape(256, QUARTER))
        ).astype(BF)

    @pl.loop(0, POINTS // 256)
    def _(n):
        at = pl.ds(pl.multiple_of(n * 256, 256), 256)
        total = jnp.zeros((128, 256), F32)
        for r in range(ROWS):
            total += dot_t(rows[r * 128 : (r + 1) * 128, :], spread_weight[r, at, :])
        est[:, at] = total

    lane = iota((8, 128), 1)

    @pl.loop(0, POINTS // 128)
    def _(n):
        at = pl.ds(pl.multiple_of(n * 128, 128), 128)
        members = [est[m * 8 : (m + 1) * 8, at] for m in range(MEMBERS)]
        total, grads = pair_terms(members, obs[:, at])
        other = pltpu.roll(total, 64, 1)
        station_out[2 * n] = jnp.where(lane < 64, total, other)
        station_out[2 * n + 1] = jnp.where(lane < 64, other, total)
        for m in range(MEMBERS):
            est[m * 8 : (m + 1) * 8, at] = grads[m]

    slopes[...] = est[...].astype(BF)


def spread_slopes(slopes, spread_weight, spread):
    for r in range(ROWS):
        @pl.loop(0, LANES // 256)
        def _(n):
            at = pl.ds(pl.multiple_of(n * 256, 256), 256)
            spread[r * 128 : (r + 1) * 128, at] = dot(slopes[...], spread_weight[r, :, at]).astype(BF)


def grid_part(received, values, truth, score):
    values[...] = received[...].astype(F32)

    @pl.loop(0, MSG // 128)
    def _(n):
        at = pl.ds(pl.multiple_of(n * 128, 128), 128)
        for half in range(2):
            part = slice(half * 8, half * 8 + 8)
            members = [values[m, part, at] for m in range(MEMBERS)]
            total, grads = pair_terms(members, truth[part, at])
            score[part, at] = total
            for m in range(MEMBERS):
                values[m, part, at] = grads[m]


def total_gradient(values, spread, grad):
    back, back_fifth = message_to_station(True)
    folded = jnp.zeros((256, QUARTER), F32)
    for q in range(4):
        at = slice(q * QUARTER, (q + 1) * QUARTER)
        total = values[:, :, at].reshape(256, QUARTER) + dot(back, spread[:, at])
        grad[:, :, at] = total.astype(BF).reshape(MEMBERS, 16, QUARTER)
        folded += dot(back_fifth[q], spread[:, at])
    total = values[:, :, LANES:].reshape(256, QUARTER) + folded
    grad[:, :, LANES:] = total.astype(BF).reshape(MEMBERS, 16, QUARTER)


def unfold_score(score, score_ref):
    for r in range(ROWS):
        score_ref[r, 0:4, :] = score[4 * r : 4 * r + 4, :LON]
        for q in range(4):
            width = min(QUARTER, LON - q * QUARTER)
            score_ref[r, 4:5, q * QUARTER : q * QUARTER + width] = score[
                4 * q + r : 4 * q + r + 1, LANES : LANES + width
            ]


def own_station_scores(slot_ref, station_in, own):
    group = iota((8, 128), 1) >> 5
    even = (group & 1) == 0
    pieces = []
    for b in range(BANDS):
        here = station_in[b]
        moved = pltpu.roll(here, 32, 1)
        pieces.append(jnp.where(even, here, moved))
        pieces.append(jnp.where(even, moved, here))
    for t in range(4):
        slot = jnp.zeros((8, 128), jnp.int32)
        for g in range(4):
            slot = jnp.where(group == g, slot_ref[4 * t + g], slot)
        tile = jnp.zeros((8, 128), F32)
        for at in range(SLOTS):
            tile = jnp.where(slot == at, pieces[at], tile)
        own[:, t * 128 : (t + 1) * 128] = tile


def all_station_scores(gathered, station_ref):
    row, col = iota((128, FIELDS), 0), iota((128, FIELDS), 1)
    pick = hot(((row & 7) < 5) & ((row >> 3) * 5 + (row & 7) == col))
    whole = gathered[...].reshape(128, 512)
    high = whole.astype(BF)
    low = (whole - high.astype(F32)).astype(BF)
    dims = (((0,), (0,)), ((), ()))
    joined = lax.dot_general(high, pick, dims, preferred_element_type=F32)
    joined += lax.dot_general(low, pick, dims, preferred_element_type=F32)
    station_ref[...] = joined.reshape(16, STATIONS, FIELDS)


def state_part(returned, inverse, total, out_ref):
    main, fifth = grid_to_message(True)
    for q in range(4):
        at = slice(q * QUARTER, (q + 1) * QUARTER)
        total[:, at] = (
            dot(main, returned[:, :, at].reshape(256, QUARTER))
            + dot(fifth[q], returned[:, :, LANES:].reshape(256, QUARTER))
        ).astype(BF)
    for q in range(4):
        width = min(QUARTER, LON - q * QUARTER)
        at = slice(q * QUARTER, q * QUARTER + width)
        out_ref[0, :, :, at] = dot(total[...], inverse[:, at]).astype(BF).reshape(ROWS, FIELDS, width)


def kernel(
    start_ref, slot_ref, factor_ref, state_ref, mix_ref, share_ref, obs_ref, truth_ref, inverse_ref,
    score_ref, station_ref, out_ref,
    layers, scaled, inverse, zout, zin, weights, spread_weight, message, received, grad, returned,
    rows, est, slopes, values, spread, truth, obs, score, station_out, station_in, own, gathered, total,
    inverse_sem, halo_sem, z_sem, weight_sem, message_sem, station_sem, own_sem, grad_sem,
):
    band = lax.axis_index("band")
    member = lax.axis_index("member")
    fetch = pltpu.make_async_copy(inverse_ref, inverse, inverse_sem)
    fetch.start()

    barrier = pltpu.get_barrier_semaphore()
    u = layers.at[0]
    u[HALO : HALO + ROWS, :, LON - 32 :] = jnp.zeros((ROWS, FIELDS, LANES - LON + 32), BF)
    u[HALO : HALO + ROWS, :, :LON] = state_ref[0]

    @pl.when(band == 0)
    def _():
        u[0:HALO] = jnp.zeros((HALO, FIELDS, LANES), BF)

    @pl.when(band == BANDS - 1)
    def _():
        u[HALO + ROWS :] = jnp.zeros((HALO, FIELDS, LANES), BF)

    @pl.loop(1, 16)
    def _(step):
        for device in ({"member": member_at(member, step, 1)}, {"band": band_at(band, step, 1)}):
            pl.semaphore_signal(barrier, inc=1, device_id=device, device_id_type=pl.DeviceIdType.MESH)

    outgoing_blocks(slot_ref, share_ref, obs_ref, zout)
    pl.semaphore_wait(barrier, 30)

    def to_north(i):
        return send(u.at[HALO + ROWS - 1 - i], u.at[HALO - 1 - i], halo_sem, i, {"band": band_at(band, 1, 1)})

    def to_south(i):
        return send(u.at[HALO + i], u.at[HALO + ROWS + i], halo_sem, HALO + i, {"band": band_at(band, 1, -1)})

    for i in range(HALO):
        pl.when(band < BANDS - 1)(to_north(i).start)
        pl.when(band > 0)(to_south(i).start)

    z_args = (lambda b: zout.at[b], lambda b: zin.at[b], z_sem, band, band_at, "band")
    weight_args = (
        lambda m: zin.at[:, 0:16, :], lambda m: weights.at[m], weight_sem, member, member_at, "member"
    )
    message_args = (lambda m: message.at[m], lambda m: received.at[m], message_sem, member, member_at, "member")
    station_args = (lambda b: station_out.at[b], lambda b: station_in.at[b], station_sem, band, band_at, "band")
    own_args = (lambda m: own, lambda m: gathered.at[m], own_sem, member, member_at, "member")
    grad_args = (lambda m: grad.at[m], lambda m: returned.at[m], grad_sem, member, member_at, "member")

    exchange(*z_args)
    zin[band] = zout[band]

    def run_layer(layer, first, stop):
        @pl.loop(first, stop)
        def _(row):
            factor = band * ROWS + row
            stencil_row(
                layers.at[layer], layers.at[layer + 1], scaled, mix_ref[layer], row,
                factor_ref[factor, 0], factor_ref[factor, 1], factor_ref[factor, 2],
            )

    def run_pair(layer, low, high):
        @pl.loop(0, 2)
        def _(side):
            row = low + side * (high - low)
            factor = band * ROWS + row
            stencil_row(
                layers.at[layer], layers.at[layer + 1], scaled, mix_ref[layer], row,
                factor_ref[factor, 0], factor_ref[factor, 1], factor_ref[factor, 2],
            )

    def wait_halo(i):
        pl.when(band > 0)(to_north(i).wait_recv)
        pl.when(band < BANDS - 1)(to_south(i).wait_recv)

    run_layer(0, 4, 6)
    wait_halo(0)
    run_pair(0, 3, 6)
    wait_received(*z_args)
    exchange(*weight_args)
    weights[member] = zin[:, 0:16, :]
    wait_halo(1)
    run_pair(0, 2, 7)
    run_layer(1, 3, 7)
    wait_halo(2)
    run_pair(0, 1, 8)
    run_pair(1, 2, 7)
    run_layer(2, 3, 7)

    fetch.wait()
    diffuse_to_message(layers.at[LAYERS], inverse, message)
    exchange(*message_args)
    received[member] = message[member]

    fold_truth(truth_ref, truth)
    join_obs(zin, obs)
    wait_received(*weight_args)
    spread_out_weights(start_ref, weights, spread_weight)
    wait_received(*message_args)

    station_part(received, rows, est, slopes, spread_weight, spread, obs, station_out)
    exchange(*station_args)
    station_in[band] = station_out[band]
    spread_slopes(slopes, spread_weight, spread)
    grid_part(received, values, truth, score)
    total_gradient(values, spread, grad)
    exchange(*grad_args)
    returned[member] = grad[member]

    wait_received(*station_args)
    own_station_scores(slot_ref, station_in, own)
    exchange(*own_args)
    gathered[member] = own[...]
    unfold_score(score, score_ref)

    wait_received(*own_args)
    all_station_scores(gathered, station_ref)
    wait_received(*grad_args)
    state_part(returned, inverse, total, out_ref)

    for i in range(HALO):
        pl.when(band < BANDS - 1)(to_north(i).wait_send)
        pl.when(band > 0)(to_south(i).wait_send)
    for args in (z_args, weight_args, message_args, station_args, own_args, grad_args):
        wait_sent(*args)


def slot_tables(block_band, block_start, band_pos):
    band_table = block_band[:, 0].reshape(BANDS, -1)
    start_table = block_start.reshape(BANDS, -1)
    order = jnp.arange(band_table.shape[1], dtype=jnp.int32)
    earlier = (band_table[:, :, None] == band_table[:, None, :]) & (order[:, None] > order[None, :])
    rank_table = jnp.sum(earlier.astype(jnp.int32), axis=2)
    caps = jnp.arange(CAP, dtype=jnp.int32)
    mine = (band_table[:, None, :] == band_pos) & (rank_table[:, None, :] == caps[:, None])
    starts = jnp.sum(jnp.where(mine, start_table[:, None, :], 0), axis=2).reshape(SLOTS)
    slot_table = band_table * CAP + rank_table
    return starts, lax.dynamic_index_in_dim(slot_table, band_pos, 0, keepdims=False)


def shards(ensemble, mix_weight, analysis, station_weight, station_obs, block_band, block_start):
    band_pos = lax.axis_index("band")
    member_pos = lax.axis_index("member")
    starts, slots = slot_tables(block_band, block_start, band_pos)
    share = lax.dynamic_slice(
        station_weight, (0, (member_pos & 3) * 8, member_pos >> 2, 0), (16, 8, 1, 128)
    ).reshape(128, 128)
    obs_share = jnp.transpose(lax.dynamic_slice_in_dim(station_obs, member_pos * 5, 5, 2), (0, 2, 1))
    obs_share = jnp.tile(jnp.pad(obs_share, ((0, 0), (0, 3), (0, 0))), (1, 1, 4)).astype(F32)

    smem = pl.BlockSpec(memory_space=pltpu.SMEM)
    vmem = pl.BlockSpec(memory_space=pltpu.VMEM)
    message = (MEMBERS, 16, MSG)
    sems = pltpu.SemaphoreType.DMA((2, 16))
    return pl.pallas_call(
        kernel,
        out_shape=(
            jax.ShapeDtypeStruct((ROWS, 5, LON), F32),
            jax.ShapeDtypeStruct((16, STATIONS, FIELDS), F32),
            jax.ShapeDtypeStruct((1, ROWS, FIELDS, LON), BF),
        ),
        in_specs=[smem] * 3 + [vmem] * 5 + [pl.BlockSpec(memory_space=pl.ANY)],
        out_specs=(vmem, vmem, vmem),
        scratch_shapes=[
            pltpu.VMEM((LAYERS + 1, EXT, FIELDS, LANES), BF),
            pltpu.VMEM((FIELDS, LANES), BF),
            pltpu.VMEM((LANES, LANES), BF),
            pltpu.VMEM((BANDS, 32, 128), BF),
            pltpu.VMEM((BANDS, 32, 128), BF),
            pltpu.VMEM((MEMBERS, BANDS, 16, 128), BF),
            pltpu.VMEM((ROWS, POINTS, LANES), BF),
            pltpu.VMEM(message, BF),
            pltpu.VMEM(message, BF),
            pltpu.VMEM(message, BF),
            pltpu.VMEM(message, BF),
            pltpu.VMEM((512, LANES), BF),
            pltpu.VMEM((128, POINTS), F32),
            pltpu.VMEM((128, POINTS), BF),
            pltpu.VMEM(message, F32),
            pltpu.VMEM((512, LANES), BF),
            pltpu.VMEM((16, MSG), F32),
            pltpu.VMEM((8, POINTS), F32),
            pltpu.VMEM((16, MSG), F32),
            pltpu.VMEM((BANDS, 8, 128), F32),
            pltpu.VMEM((BANDS, 8, 128), F32),
            pltpu.VMEM((8, 512), F32),
            pltpu.VMEM((MEMBERS, 8, 512), F32),
            pltpu.VMEM((ROWS * FIELDS, LANES), BF),
            pltpu.SemaphoreType.DMA,
            sems, sems, sems, sems, sems, sems, sems,
        ],
        compiler_params=pltpu.CompilerParams(
            vmem_limit_bytes=56 * MIB, collective_id=0, has_side_effects=True
        ),
    )(
        starts, slots, jnp.asarray(row_factors()), ensemble, mix_weight, share, obs_share, analysis,
        jnp.asarray(inverse_table()),
    )


def solution(mesh):
    return jax.shard_map(
        shards,
        mesh=mesh,
        in_specs=(
            P("member", "band", None, None),
            P(),
            P("band", "member", None),
            P("band", None, None, None),
            P("band", None, None),
            P(),
            P(),
        ),
        out_specs=(
            P("band", "member", None),
            P("band", None, None),
            P("member", "band", None, None),
        ),
        check_vma=False,
    )
```

time: 795 us -> 113 us (0.14)
  other arithmetic: 304 us -> 2.52 us
  waiting for transfers between devices: 150 us -> 0 us
  local copies, waits for them, and re-layouts: 145 us -> 11.8 us
  Pallas kernels: 0 us -> 96.8 us
  loops' own time: 61.3 us -> 0 us
  blocking collectives: 42.2 us -> 0 us
  starting transfers between devices: 35.9 us -> 0 us
  matrix products: 31.7 us -> 0 us
  between operations: 15 us -> 0.7 us
    add x65 -> x0, other arithmetic: 286 us -> none  [the longest x16 165 us: station_step(): partial_value[1] + kernel_slope(spread)]
    unnamed x4 -> x0, waiting for transfers between devices: 97.6 us -> none
    pallas_call x0 -> x1, Pallas kernels: none -> 96.8 us  [shards(): pl.pallas_call(kernel, out_shape=(jax.ShapeDtypeStruct((ROWS, 5, LON), F3...]
    dynamic_update_slice x32 -> x0, local copies, waits for them, and re-layouts: 65.1 us -> none  [place_slot(): lax.dynamic_update_slice_in_dim(running, existing + piece, first_lon, 2)]
    another operation x3 -> x0, loops' own time: 61.3 us -> none  [the longest x1 61.2 us: shards(): lax.fori_loop(0, slot_count, place_slot, jnp.zeros(diffused.shape, jnp.fl...]
    all_gather x2 -> x0, waiting for transfers between devices: 45.2 us -> none  [the longest x1 45.2 us: shards(): lax.all_gather(own_blocks[None].astype(jnp.bfloat16), 'member', axis=0, t...]
    dot_general x6 -> x0, matrix products: 31.7 us -> none  [the longest x1 9.78 us: shards(): jnp.dot(current.reshape(-1, points), inverse, preferred_element_type=jnp....]
    all_gather x1 -> x0, blocking collectives: 22.2 us -> none  [shards(): lax.all_gather(analysis, 'member', axis=1, tiled=True).astype(jnp.float32)]
  transfers between devices with their start and end apart: 11 -> 0, of which waited for: 5 -> 0; matrix products, arithmetic and copies ran while one was open for 49% -> 0% of each run, Pallas kernels for 0% -> 0%
where the time goes in v1:
time: 113 us; the launch traced here: 112 us
  Pallas kernels  96.8 us (86%)
  local copies, waits for them, and re-layouts  11.8 us (10%)
  other arithmetic  2.52 us (2%)
    pallas_call x1, Pallas kernels, shards(): pl.pallas_call(kernel, out_shape=(jax.ShapeDtypeStruct((ROWS, 5, LON), F3...  96.8 us
    unnamed x8, local copies, waits for them, and re-layouts  6.67 us

profile of v1, /device:TPU:1, one launch (start us, length us, event | category | flops | bytes accessed | tf_op | source)
XLA Modules:
  0.0 111.8 jit_solution(13069170103154000552)
XLA Ops:
  0.6 0.0 copy-start
  0.7 0.5 broadcast.20
  1.2 1.3 %reduce.3 = s32[256]{0:T(256)S(1)} reduce(s32[256,1]{0,1:T(1,128)} %param.14, s32[]{:T(128)} %broadcast.20), dimensions={1}, to_apply=%param.14.reduce_sub_computation.3 | reduce | bytes 2052 | tf_op args[5]
  2.5 0.1 broadcast_in_dim_reshape_squeeze.2
  2.6 0.4 convert_reduce_fusion
  3.0 0.6 fusion.2.slot_ref
  3.6 0.8 broadcast_in_dim.18
  4.4 0.1 select_reduce_fusion
  4.5 0.1 copy.24
  4.6 0.6 reshape.40.start_ref
  5.2 0.0 copy-done
  5.2 0.1 constant_dynamic-slice_fusion.2
  5.3 0.6 copy.32
  5.9 1.5 %copy.27.truth_ref = bf16[4,5,1440]{2,1,0:T(8,128)(2,1)} copy(bf16[4,5,1440]{2,0,1:T(4,128)(2,1)} %param.11) | data formatting | bytes 115200 | tf_op args[2]
  7.4 1.0 constant_dynamic-slice_fusion.1
  8.4 0.2 copy.30
  8.6 0.1 tile.2
  8.7 0.8 convert_element_type.12.obs_ref
  9.5 96.8 %shard_map.112 = (f32[4,5,1440]{2,1,0:T(8,128)}, f32[16,32,80]{2,1,0:T(8,128)}, bf16[1,4,80,1440]{3,2,1,0:T(8,128)(2,1)}) custom-call(s32[32]{0:T(128)} %reshape.40.start_ref, s32[16]{0:T(128)} %fusion.2.slot_ref, f32[70,3]{1,0:T(8,128)} %constant.35.clone.factor_ref, bf16[1,4,80,1440]{3,2,1,0:T(8,128)(2,1)} %state_ref.1, bf16[3,80,80]{2,1,0:T(8,128)(2,1)} %mix_ref.1, ...), custom_call_target="tpu_custom_call" | custom-call | tf_op jit(solution)/shard_map/pallas_call | solution.py:534
  106.3 1.7 %copy.28 = f32[4,5,1440]{2,0,1:T(4,128)} copy(f32[4,5,1440]{2,1,0:T(8,128)} %get-tuple-element.12) | data formatting | bytes 230400 | tf_op jit(solution)/shard_map/pallas_call | solution.py:534
  108.0 1.7 %copy.35 = f32[16,32,80]{2,1,0:T(8,128)} copy(f32[16,32,80]{2,1,0:T(8,128)} %get-tuple-element.19) | data formatting | bytes 327680
  109.6 2.2 %copy.36 = bf16[1,4,80,1440]{3,2,1,0:T(8,128)(2,1)} copy(bf16[1,4,80,1440]{3,2,1,0:T(8,128)(2,1)} %get-tuple-element.20) | data formatting | bytes 1843200
  (3 shorter events, 0.0 us)
Async XLA Ops:
  0.6 4.6 %copy-start = (bf16[16,32,4,128]{3,2,1,0:T(4,128)(2,1)S(1)}, bf16[16,32,4,128]{3,2,1,0:T(4,128)(2,1)}, u32[]{:S(2)}) copy-start(bf16[16,32,4,128]{3,2,1,0:T(4,128)(2,1)} %param.12) | copy-start | bytes 1572868

commit v2 on v1

v2 whole, which is shorter than its diff:
```python
import math

import jax
import jax.numpy as jnp
import numpy as np
from jax import lax
from jax.experimental import pallas as pl
from jax.experimental.pallas import tpu as pltpu
from jax.sharding import PartitionSpec as P

CAP = 2
DIFFUSION = 4.0

ROWS = 4
HALO = 3
EXT = ROWS + 2 * HALO
FIELDS = 80
LON = 1440
LANES = 1536
CHUNKS = 3
CHUNK = LANES // CHUNKS
TILES = CHUNK // 128
PIECE = CHUNK + 128
MEMBERS = 16
BANDS = 16
TOTAL_ROWS = 64
LAYERS = 3
SLOTS = BANDS * CAP
STATIONS = 32
POINTS = SLOTS * STATIONS
PAIRS = MEMBERS * (MEMBERS - 1) // 2
MIB = 1 << 20

BF = jnp.bfloat16
F32 = jnp.float32


def inverse_table():
    centre = 1.0 + 2.0 * DIFFUSION
    root = (centre - math.sqrt(centre * centre - 4.0 * DIFFUSION * DIFFUSION)) / (2.0 * DIFFUSION)
    factor = 1.0 / (DIFFUSION * (1.0 / root - root) * (1.0 - root**LON))
    offset = np.abs(np.arange(LON)[:, None] - np.arange(LON)[None, :])
    nearest = np.minimum(offset, LON - offset).astype(np.float64)
    values = (np.exp(nearest * math.log(root)) + np.exp((LON - nearest) * math.log(root))) * factor
    table = np.zeros((LANES, LANES), np.float32)
    table[:LON, :LON] = values
    return table.astype(BF)


def row_factors():
    rows = np.arange(-HALO, TOTAL_ROWS + HALO)
    cosine = np.cos(math.pi * ((rows + 0.5) / TOTAL_ROWS - 0.5))
    metric = 1.0 / (cosine * cosine + 0.1)
    inside = (rows >= 0) & (rows < TOTAL_ROWS)
    return np.stack([metric / (2 + 2 * metric), 1 / (2 + 2 * metric), inside], axis=1).astype(np.float32)


def hot(condition):
    return jnp.where(condition, 1.0, 0.0).astype(BF)


def iota(shape, dim):
    return lax.broadcasted_iota(jnp.int32, shape, dim)


def grid_to_message(transposed):
    shape = (320, 256) if transposed else (256, 320)
    row, col = iota(shape, int(transposed)), iota(shape, 1 - int(transposed))
    group, place = row >> 4, row & 15
    main = hot(col == (place >> 2) * FIELDS + group * 5 + (place & 3))
    fifth = col == (place & 3) * FIELDS + group * 5 + 4
    return main, [hot(fifth & ((place >> 2) == t)) for t in range(TILES)]


def message_to_station(transposed):
    shape = (256, 512) if transposed else (512, 256)
    row, col = iota(shape, int(transposed)), iota(shape, 1 - int(transposed))
    r, member, f = row >> 7, (row >> 3) & 15, row & 7
    same = member == (col >> 4)
    place = col & 15
    main = hot(same & (f < 4) & (place == r * 4 + f))
    return main, [hot(same & (f == 4) & (place == t * 4 + r)) for t in range(TILES)]


def lane_tile(t):
    return slice(t * 128, (t + 1) * 128)


def lane_chunk(q):
    return slice(q * CHUNK, (q + 1) * CHUNK)


def dot(a, b):
    return jnp.dot(a, b, preferred_element_type=F32)


def dot_t(a, b):
    return lax.dot_general(a, b, (((1,), (1,)), ((), ())), preferred_element_type=F32)


def stencil_row(u, nxt, weight, row, east_west, north_south, inside):
    tiles = LANES // 128
    lane = iota((FIELDS, 128), 1)

    def tile(at, t):
        return u[at, :, t * 128 : (t + 1) * 128].astype(F32)

    first, last = tile(row, 0), tile(row, tiles - 1)
    wrapped = jnp.where(lane == LON % 128, pltpu.roll(first, LON % 128, 1), last)
    before = pltpu.roll(last, 129 - LON % 128, 1)
    here = first
    ahead = pltpu.roll(here, 127, 1)
    for pair in range(tiles // 2):
        values, middles = [], []
        for t in (2 * pair, 2 * pair + 1):
            after = wrapped if t == tiles - 2 else (tile(row, t + 1) if t < tiles - 1 else here)
            further = pltpu.roll(after, 127, 1) if t < tiles - 1 else ahead
            east = jnp.where(lane == 127, further, ahead)
            moved = pltpu.roll(here, 1, 1)
            west = jnp.where(lane == 0, before, moved)
            sides = tile(row - 1, t) + tile(row + 1, t)
            values.append((east + west) * east_west + sides * north_south - here)
            middles.append(here)
            before, here, ahead = moved, after, further
        mixed = dot(weight, jnp.concatenate(values, axis=1).astype(BF))
        fresh = jnp.concatenate(middles, axis=1) + jnp.tanh(mixed)
        if inside is not None:
            fresh = fresh * inside
        nxt[row, :, pair * 256 : (pair + 1) * 256] = fresh.astype(BF)


def diffuse_chunk(q, rows, inverse, main, fifth, message):
    piece = dot(rows, inverse[:, lane_chunk(q)]).astype(BF)
    message[q, :, :, :CHUNK] = dot(main, piece).astype(BF).reshape(MEMBERS, 16, CHUNK)
    below = sum(dot(fifth[t], piece[:, lane_tile(t)]) for t in range(TILES))
    message[q, :, :, CHUNK:] = below.astype(BF).reshape(MEMBERS, 16, 128)


def pair_terms(values, truth):
    slopes = [None] * MEMBERS
    total = None
    for i in range(MEMBERS):
        for j in range(i + 1, MEMBERS):
            spread = values[i] - values[j]
            square = spread * spread + 1.0
            inverse = lax.rsqrt(square)
            slope = spread * inverse
            root = square * inverse
            total = root if total is None else total + root
            slopes[i] = slope if slopes[i] is None else slopes[i] + slope
            slopes[j] = -slope if slopes[j] is None else slopes[j] - slope
    error_total = None
    grads = []
    for m in range(MEMBERS):
        error = values[m] - truth
        square = error * error + 1.0
        inverse = lax.rsqrt(square)
        root = square * inverse
        error_total = root if error_total is None else error_total + root
        grads.append(error * inverse - slopes[m] * (1.0 / (MEMBERS - 1)))
    score = (error_total - MEMBERS) * (1.0 / MEMBERS) - (total - PAIRS) * (1.0 / (MEMBERS * (MEMBERS - 1)))
    return score, grads


def send(src, dst, sems, at, device):
    return pltpu.make_async_remote_copy(
        src_ref=src,
        dst_ref=dst,
        send_sem=sems.at[0, at],
        recv_sem=sems.at[1, at],
        device_id=device,
        device_id_type=pl.DeviceIdType.MESH,
    )


def member_at(member, step, sign):
    x = (member + sign * (step & 3)) & 3
    y = ((member >> 2) + sign * (step >> 2)) & 3
    return y * 4 + x


def band_at(band, step, sign):
    return (band + sign * step) & (BANDS - 1)


def exchange(source, target, sems, me, at, axis):
    @pl.loop(1, 16)
    def _(step):
        peer = at(me, step, 1)
        send(source(peer), target(me), sems, step, {axis: peer}).start()


def wait_received(source, target, sems, me, at, axis):
    @pl.loop(1, 16)
    def _(step):
        peer = at(me, step, -1)
        send(source(peer), target(peer), sems, step, {axis: peer}).wait_recv()


def wait_sent(source, target, sems, me, at, axis):
    @pl.loop(1, 16)
    def _(step):
        peer = at(me, step, 1)
        send(source(peer), target(me), sems, step, {axis: peer}).wait_send()


def find_slots(band_ref, band, slot_ref):
    own = [band_ref[band * 16 + k] for k in range(16)]
    for k in range(16):
        rank = jnp.int32(0)
        for i in range(k):
            rank += jnp.where(own[i] == own[k], 1, 0)
        slot_ref[k] = own[k] * CAP + rank


def find_starts(band_ref, first_ref, band, start_ref):
    @pl.loop(0, BANDS)
    def _(home):
        seen, first, second = jnp.int32(0), jnp.int32(0), jnp.int32(0)
        for k in range(16):
            match = band_ref[home * 16 + k] == band
            here = first_ref[home * 16 + k]
            first = jnp.where(match & (seen == 0), here, first)
            second = jnp.where(match & (seen == 1), here, second)
            seen += jnp.where(match, 1, 0)
        start_ref[home * CAP] = first
        start_ref[home * CAP + 1] = second


def outgoing_shares(slot_ref, weight_ref, member, zout):
    row, col = iota((8, 128), 0), iota((8, 128), 1)
    own = hot(col == (16 + (member & 1) * 8 + row) * ROWS + ((member >> 1) & 3))
    share = jnp.concatenate([dot(own, weight_ref[k]) for k in range(16)], axis=0).astype(BF)
    lane = iota((1, 128), 1)
    slot_row = jnp.zeros((1, 128), jnp.int32)
    for k in range(16):
        slot_row = jnp.where((lane >> 3) == k, slot_ref[k], slot_row)
    row, col = iota((128, 128), 0), iota((128, 128), 1)
    pick = hot(((row >> 3) * CAP + (member >> 3) == slot_row) & ((row & 7) == (col & 7)))
    picked = dot(pick, share)
    for b in range(BANDS):
        zout[b] = jnp.concatenate([picked[b * 8 : b * 8 + 8], jnp.zeros((8, 128), F32)], axis=0).astype(BF)


def join_shares(zin, joined):
    for pair in range(BANDS // 2):
        parts = [zin[2 * pair + odd].astype(F32)[0:8] for odd in range(2)]
        joined[pair] = jnp.concatenate(parts, axis=0).astype(BF)


def outgoing_direct(slot_ref, weight_ref, turned, direct_out):
    row, col = iota((64, 128), 0), iota((64, 128), 1)
    pick = hot(col == (row & 15) * ROWS + (row >> 4))
    for k in range(16):
        turned[k] = dot(pick, weight_ref[k]).astype(BF)

    @pl.loop(0, BANDS)
    def _(b):
        for cap in range(CAP):
            block = jnp.zeros((64, 128), BF)
            for k in range(16):
                block = jnp.where(jnp.full((64, 128), slot_ref[k], jnp.int32) == b * CAP + cap, turned[k], block)
            direct_out[b, cap * 64 : (cap + 1) * 64, :] = block


def outgoing_obs(slot_ref, obs_ref, member, obs_out):
    row, col = iota((16, FIELDS), 0), iota((16, FIELDS), 1)
    pick = hot((row < 5) & (col == member * 5 + row))
    own = dot_t(pick, obs_ref[...].reshape(16 * STATIONS, FIELDS))[0:8]
    group = iota((8, 128), 1) >> 5
    blocks = []
    for k in range(16):
        block = jnp.where(group == (k & 3), own[:, lane_tile(k >> 2)], 0.0)
        block += pltpu.roll(block, 32, 1)
        blocks.append(block + pltpu.roll(block, 64, 1))
    for t in range(SLOTS // 4):
        tile = jnp.zeros((8, 128), F32)
        for k in range(16):
            tile = jnp.where(group + 4 * t == slot_ref[k], blocks[k], tile)
        for odd in range(2):
            piece = pltpu.roll(tile, 64, 1) if odd else tile
            obs_out[2 * t + odd] = jnp.concatenate([piece, jnp.zeros((8, 128), F32)], axis=0).astype(BF)


def spread_out_weights(start_ref, direct, weights, spread_weight):
    lane = iota((STATIONS, 128), 1)

    @pl.loop(0, BANDS // 2)
    def _(pair):
        for cap in range(CAP):
            shares = [
                [weights[cap * 8 + r * 2 + g, pair].astype(F32) for g in range(2)] for r in range(ROWS)
            ]
            for odd in range(2):
                home = pair * 2 + odd
                start = start_ref[home * CAP + cap]
                shift = start & 127
                at = pl.ds(home * 64 + cap * STATIONS, STATIONS)
                moved = []
                for r in range(ROWS):
                    near = direct[home, cap * 64 + r * 16 : cap * 64 + r * 16 + 16, :].astype(F32)
                    passed = [share[odd * 8 : odd * 8 + 8] for share in shares[r]]
                    moved.append(pltpu.roll(jnp.concatenate([near] + passed, axis=0), shift, 1))
                for t in range(LANES // 128):
                    place = lane + t * 128 - start
                    inside = (place >= 0) & (place < 128)
                    for r in range(ROWS):
                        spread_weight[r, at, lane_tile(t)] = jnp.where(inside, moved[r], 0.0).astype(BF)


def fold_truth(truth_ref, truth):
    truth[...] = jnp.zeros((CHUNKS, 16, PIECE), F32)
    fields = [truth_ref[f].astype(F32) for f in range(5)]
    for q in range(CHUNKS):
        width = min(CHUNK, LON - q * CHUNK)
        for r in range(ROWS):
            for f in range(4):
                truth[q, 4 * r + f : 4 * r + f + 1, :width] = fields[f][r : r + 1, q * CHUNK : q * CHUNK + width]
        for t in range(TILES):
            first = q * CHUNK + t * 128
            width = min(128, LON - first)
            truth[q, 4 * t : 4 * t + 4, CHUNK : CHUNK + width] = fields[4][:, first : first + width]


def unfold_score(score, score_ref):
    for q in range(CHUNKS):
        width = min(CHUNK, LON - q * CHUNK)
        for r in range(ROWS):
            for f in range(4):
                score_ref[f, r : r + 1, q * CHUNK : q * CHUNK + width] = score[
                    q, 4 * r + f : 4 * r + f + 1, :width
                ]
        for t in range(TILES):
            first = q * CHUNK + t * 128
            width = min(128, LON - first)
            score_ref[4, :, first : first + width] = score[q, 4 * t : 4 * t + 4, CHUNK : CHUNK + width]


def join_obs(obs_in, obs):
    lane = iota((8, 128), 1)
    for t in range(POINTS // 128):
        low = obs_in[2 * t].astype(F32)[0:8]
        high = obs_in[2 * t + 1].astype(F32)[0:8]
        obs[:, lane_tile(t)] = jnp.where(lane < 64, low, pltpu.roll(high, 64, 1))


def station_rows(q, received, main, fifth, rows):
    for t in range(TILES):
        tile = dot(main, received[q, :, :, lane_tile(t)].reshape(256, 128))
        tile += dot(fifth[t], received[q, :, :, CHUNK:].reshape(256, 128))
        rows[:, lane_tile(q * TILES + t)] = tile.astype(BF)


def estimates(first, stop, rows, spread_weight, est):
    for r in range(ROWS):
        part = dot_t(rows[r * 128 : (r + 1) * 128, first:stop], spread_weight[r, :, first:stop])
        est[...] = part if r == 0 and first == 0 else est[...] + part


def station_scores(est, slopes, obs, station_out):
    lane = iota((8, 128), 1)

    @pl.loop(0, POINTS // 256)
    def _(n):
        for half in range(2):
            at = pl.ds(pl.multiple_of(n * 256 + half * 128, 128), 128)
            members = [est[m * 8 : (m + 1) * 8, at] for m in range(MEMBERS)]
            total, grads = pair_terms(members, obs[:, at])
            other = pltpu.roll(total, 64, 1)
            station_out[4 * n + 2 * half] = jnp.where(lane < 64, total, other)
            station_out[4 * n + 2 * half + 1] = jnp.where(lane < 64, other, total)
            for m in range(0, MEMBERS, 2):
                slopes[m * 8 : m * 8 + 16, at] = jnp.concatenate(grads[m : m + 2], axis=0).astype(BF)


def grid_pairs(q, received, values, truth, score):
    values[q] = received[q].astype(F32)

    @pl.loop(0, PIECE // 128)
    def _(n):
        at = pl.ds(pl.multiple_of(n * 128, 128), 128)
        for half in range(2):
            part = slice(half * 8, half * 8 + 8)
            members = [values[q, m, part, at] for m in range(MEMBERS)]
            total, grads = pair_terms(members, truth[q, part, at])
            score[q, part, at] = total
            for m in range(MEMBERS):
                values[q, m, part, at] = grads[m]


def spread_chunk(q, slopes, spread_weight, spread):
    for r in range(ROWS):
        part = dot(slopes[...], spread_weight[r, :, lane_chunk(q)])
        spread[r * 128 : (r + 1) * 128, :] = part.astype(BF)


def total_chunk(q, values, spread, back, back_fifth, grad):
    total = values[q, :, :, :CHUNK].reshape(256, CHUNK) + dot(back, spread[...])
    grad[q, :, :, :CHUNK] = total.astype(BF).reshape(MEMBERS, 16, CHUNK)
    below = values[q, :, :, CHUNK:].reshape(256, 128)
    for t in range(TILES):
        below += dot(back_fifth[t], spread[:, lane_tile(t)])
    grad[q, :, :, CHUNK:] = below.astype(BF).reshape(MEMBERS, 16, 128)


def own_station_scores(slot_ref, station_in, own):
    group = iota((8, 128), 1) >> 5
    even = (group & 1) == 0
    pieces = []
    for b in range(BANDS):
        here = station_in[b]
        moved = pltpu.roll(here, 32, 1)
        pieces.append(jnp.where(even, here, moved))
        pieces.append(jnp.where(even, moved, here))
    tiles = []
    for t in range(4):
        slot = jnp.zeros((8, 128), jnp.int32)
        for g in range(4):
            slot = jnp.where(group == g, slot_ref[4 * t + g], slot)
        tile = jnp.zeros((8, 128), F32)
        for at in range(SLOTS):
            tile = jnp.where(slot == at, pieces[at], tile)
        tiles.append(tile)
    for t in range(2):
        own[:, lane_tile(t)] = jnp.concatenate([tiles[t], tiles[t + 2]], axis=0).astype(BF)


def all_station_scores(gathered, station_ref):
    row, col = iota((256, FIELDS), 0), iota((256, FIELDS), 1)
    field = (row >> 4) * 5 + (row & 7)
    whole = gathered[...].reshape(256, 256)
    dims = (((0,), (0,)), ((), ()))
    for half in range(2):
        pick = hot(((row & 7) < 5) & (field == col) & (((row >> 3) & 1) == half))
        joined = lax.dot_general(whole, pick, dims, preferred_element_type=F32)
        station_ref[half * 8 : half * 8 + 8] = joined.reshape(8, STATIONS, FIELDS)


def add_state(q, returned, main, fifth, inverse, total, state, out, copies):
    for t in range(TILES):
        tile = dot(main, returned[q, :, :, lane_tile(t)].reshape(256, 128))
        tile += dot(fifth[t], returned[q, :, :, CHUNK:].reshape(256, 128))
        total[:, lane_tile(t)] = tile.astype(BF)
    for n in range(CHUNKS):
        width = min(CHUNK, LON - n * CHUNK)
        at = slice(n * CHUNK, n * CHUNK + width)
        part = dot(total[...], inverse[lane_chunk(q), at])
        if q > 0:
            part += state[:, at]
        if q < CHUNKS - 1:
            state[:, at] = part
        else:
            out[0, :, :, at] = part.astype(BF).reshape(ROWS, FIELDS, width)
            copies[n].start()


def kernel(
    band_ref, first_ref, factor_ref, state_hbm, mix_ref, weight_hbm, obs_hbm, truth_hbm, inverse_hbm,
    score_ref, station_ref, out_ref,
    start_ref, slot_ref,
    state_ref, weight_ref, obs_ref, truth_ref,
    layers, inverse, zout, zin, joined, turned, direct_out, direct_in, obs_out, obs_in, weights, spread_weight, message, received, grad, returned,
    rows, est, slopes, values, spread, truth, obs, score, station_out, station_in, own, gathered,
    total, state, score_out, scores_out, out,
    fetch_sem, leave_sem, halo_sem, z_sem, obs_sem, direct_sem, weight_sem, message_sem, station_sem, own_sem, grad_sem,
):
    band = lax.axis_index("band")
    member = lax.axis_index("member")
    barrier = pltpu.get_barrier_semaphore()

    @pl.loop(1, 16)
    def _(step):
        for device in ({"member": member_at(member, step, 1)}, {"band": band_at(band, step, 1)}):
            pl.semaphore_signal(barrier, inc=1, device_id=device, device_id_type=pl.DeviceIdType.MESH)

    fetches = [
        pltpu.make_async_copy(source, target, fetch_sem.at[i])
        for i, (source, target) in enumerate(
            [(state_hbm.at[0, r], state_ref.at[0, r]) for r in range(ROWS)]
            + [
                (weight_hbm, weight_ref), (obs_hbm, obs_ref), (truth_hbm, truth_ref),
                (inverse_hbm, inverse),
            ]
        )
    ]
    for fetch in fetches:
        fetch.start()

    u = layers.at[0]
    u[HALO : HALO + ROWS, :, LON - 32 :] = jnp.zeros((ROWS, FIELDS, LANES - LON + 32), BF)

    @pl.when(band == 0)
    def _():
        u[0:HALO] = jnp.zeros((HALO, FIELDS, LANES), BF)

    @pl.when(band == BANDS - 1)
    def _():
        u[HALO + ROWS :] = jnp.zeros((HALO, FIELDS, LANES), BF)

    find_slots(band_ref, band, slot_ref)
    for fetch in fetches[:ROWS]:
        fetch.wait()
    u[HALO : HALO + ROWS, :, :LON] = state_ref[0]

    def to_north(i):
        return send(u.at[HALO + ROWS - 1 - i], u.at[HALO - 1 - i], halo_sem, i, {"band": band_at(band, 1, 1)})

    def to_south(i):
        return send(u.at[HALO + i], u.at[HALO + ROWS + i], halo_sem, HALO + i, {"band": band_at(band, 1, -1)})

    def send_halo(i):
        pl.when(band < BANDS - 1)(to_north(i).start)
        pl.when(band > 0)(to_south(i).start)

    direct_args = (lambda b: direct_out.at[b], lambda b: direct_in.at[b], direct_sem, band, band_at, "band")
    weight_args = (lambda m: joined, lambda m: weights.at[m], weight_sem, member, member_at, "member")
    z_args = (lambda b: zout.at[b], lambda b: zin.at[b], z_sem, band, band_at, "band")
    obs_args = (lambda b: obs_out.at[b], lambda b: obs_in.at[b], obs_sem, band, band_at, "band")
    station_args = (lambda b: station_out.at[b], lambda b: station_in.at[b], station_sem, band, band_at, "band")
    own_args = (lambda m: own, lambda m: gathered.at[m], own_sem, member, member_at, "member")

    def message_args(q):
        return (
            lambda m: message.at[q, m], lambda m: received.at[q, m], message_sem.at[q], member, member_at, "member"
        )

    def grad_args(q):
        return lambda m: grad.at[q, m], lambda m: returned.at[q, m], grad_sem.at[q], member, member_at, "member"

    def run_pair(layer, low, high):
        own = HALO <= low and high < HALO + ROWS

        @pl.loop(0, 2)
        def _(side):
            row = low + side * (high - low)
            factor = band * ROWS + row
            stencil_row(
                layers.at[layer], layers.at[layer + 1], mix_ref[layer], row,
                factor_ref[factor, 0], factor_ref[factor, 1], None if own else factor_ref[factor, 2],
            )

    def wait_halo(i):
        pl.when(band > 0)(to_north(i).wait_recv)
        pl.when(band < BANDS - 1)(to_south(i).wait_recv)

    run_pair(0, 4, 5)
    fetches[ROWS].wait()
    pl.semaphore_wait(barrier, 30)
    send_halo(0)
    outgoing_shares(slot_ref, weight_ref, member, zout)
    exchange(*z_args)
    send_halo(1)
    send_halo(2)
    zin[band] = zout[band]
    fetches[ROWS + 1].wait()
    outgoing_obs(slot_ref, obs_ref, member, obs_out)
    obs_in[band] = obs_out[band]
    outgoing_direct(slot_ref, weight_ref, turned, direct_out)
    direct_in[band] = direct_out[band]
    find_starts(band_ref, first_ref, band, start_ref)
    fetches[ROWS + 2].wait()
    fold_truth(truth_ref, truth)
    wait_halo(0)
    run_pair(0, 3, 6)
    wait_received(*z_args)
    join_shares(zin, joined)
    exchange(*weight_args)
    weights[member] = joined[...]
    run_pair(1, 4, 5)
    wait_halo(1)
    exchange(*obs_args)
    exchange(*direct_args)
    run_pair(0, 2, 7)
    run_pair(1, 3, 6)
    run_pair(2, 4, 5)
    wait_halo(2)
    run_pair(0, 1, 8)
    run_pair(1, 2, 7)
    run_pair(2, 3, 6)

    fetches[ROWS + 3].wait()
    main, fifth = grid_to_message(False)
    grid_rows = layers[LAYERS, HALO : HALO + ROWS].reshape(ROWS * FIELDS, LANES)
    for q in range(CHUNKS):
        diffuse_chunk(q, grid_rows, inverse, main, fifth, message)
        exchange(*message_args(q))
        received[q, member] = message[q, member]

    main, fifth = message_to_station(False)
    for q in range(CHUNKS - 1):
        wait_received(*message_args(q))
        station_rows(q, received, main, fifth, rows)
        grid_pairs(q, received, values, truth, score)
        if q == 0:
            wait_received(*obs_args)
            join_obs(obs_in, obs)
            wait_received(*weight_args)
            wait_received(*direct_args)
            spread_out_weights(start_ref, direct_in, weights, spread_weight)

    estimates(0, CHUNK * (CHUNKS - 1), rows, spread_weight, est)
    wait_received(*message_args(CHUNKS - 1))
    station_rows(CHUNKS - 1, received, main, fifth, rows)
    estimates(CHUNK * (CHUNKS - 1), LANES, rows, spread_weight, est)
    station_scores(est, slopes, obs, station_out)
    exchange(*station_args)
    station_in[band] = station_out[band]

    def share_station_scores():
        wait_received(*station_args)
        own_station_scores(slot_ref, station_in, own)
        exchange(*own_args)
        gathered[member] = own[...]

    back, back_fifth = message_to_station(True)
    for q in range(CHUNKS):
        spread_chunk(q, slopes, spread_weight, spread)
        if q == CHUNKS - 1:
            grid_pairs(q, received, values, truth, score)
        total_chunk(q, values, spread, back, back_fifth, grad)
        exchange(*grad_args(q))
        returned[q, member] = grad[q, member]

    leave = [
        pltpu.make_async_copy(score_out, score_ref, leave_sem.at[0]),
        pltpu.make_async_copy(scores_out, station_ref, leave_sem.at[1]),
    ]
    leave_state = []
    for n in range(CHUNKS):
        at = slice(n * CHUNK, min((n + 1) * CHUNK, LON))
        leave_state.append(pltpu.make_async_copy(out.at[:, :, :, at], out_ref.at[:, :, :, at], leave_sem.at[2 + n]))
    unfold_score(score, score_out)
    leave[0].start()
    share_station_scores()
    for i in range(HALO):
        pl.when(band < BANDS - 1)(to_north(i).wait_send)
        pl.when(band > 0)(to_south(i).wait_send)
    for args in (obs_args, z_args, direct_args, weight_args, station_args):
        wait_sent(*args)
    for q in range(CHUNKS):
        wait_sent(*message_args(q))

    main, fifth = grid_to_message(True)
    for q in range(CHUNKS):
        wait_received(*grad_args(q))
        add_state(q, returned, main, fifth, inverse, total, state, out, leave_state)
        wait_sent(*grad_args(q))
    wait_received(*own_args)
    all_station_scores(gathered, scores_out)
    leave[1].start()
    wait_sent(*own_args)
    for copy in leave:
        copy.wait()
    for copy in leave_state:
        copy.wait()


def hand_over(*refs):
    count = len(refs) // 2
    for i in range(count):
        refs[count + i][...] = refs[i][...]


def shards(ensemble, mix_weight, analysis, station_weight, station_obs, block_band, block_start):
    smem = pl.BlockSpec(memory_space=pltpu.SMEM)
    vmem = pl.BlockSpec(memory_space=pltpu.VMEM)
    anywhere = pl.BlockSpec(memory_space=pl.ANY)
    message = (CHUNKS, MEMBERS, 16, PIECE)
    sems = pltpu.SemaphoreType.DMA((2, 16))
    piece_sems = pltpu.SemaphoreType.DMA((CHUNKS, 2, 16))
    shapes = (
        jax.ShapeDtypeStruct((5, ROWS, LON), F32),
        jax.ShapeDtypeStruct((16, STATIONS, FIELDS), F32),
        jax.ShapeDtypeStruct((1, ROWS, FIELDS, LON), BF),
    )
    outs = pl.pallas_call(
        kernel,
        out_shape=tuple(pltpu.VMEM(shape.shape, shape.dtype) for shape in shapes),
        in_specs=[smem] * 3 + [anywhere, vmem] + [anywhere] * 4,
        out_specs=(anywhere,) * 3,
        scratch_shapes=[
            pltpu.SMEM((SLOTS,), jnp.int32),
            pltpu.SMEM((16,), jnp.int32),
            pltpu.VMEM((1, ROWS, FIELDS, LON), BF),
            pltpu.VMEM((16, STATIONS * ROWS, 128), BF),
            pltpu.VMEM((16, STATIONS, FIELDS), BF),
            pltpu.VMEM((5, ROWS, LON), BF),
            pltpu.VMEM((LAYERS + 1, EXT, FIELDS, LANES), BF),
            pltpu.VMEM((LANES, LANES), BF),
            pltpu.VMEM((BANDS, 16, 128), BF),
            pltpu.VMEM((BANDS, 16, 128), BF),
            pltpu.VMEM((BANDS // 2, 16, 128), BF),
            pltpu.VMEM((16, 64, 128), BF),
            pltpu.VMEM((BANDS, 128, 128), BF),
            pltpu.VMEM((BANDS, 128, 128), BF),
            pltpu.VMEM((BANDS, 16, 128), BF),
            pltpu.VMEM((BANDS, 16, 128), BF),
            pltpu.VMEM((MEMBERS, BANDS // 2, 16, 128), BF),
            pltpu.VMEM((ROWS, POINTS, LANES), BF),
            pltpu.VMEM(message, BF),
            pltpu.VMEM(message, BF),
            pltpu.VMEM(message, BF),
            pltpu.VMEM(message, BF),
            pltpu.VMEM((512, LANES), BF),
            pltpu.VMEM((128, POINTS), F32),
            pltpu.VMEM((128, POINTS), BF),
            pltpu.VMEM(message, F32),
            pltpu.VMEM((512, CHUNK), BF),
            pltpu.VMEM((CHUNKS, 16, PIECE), F32),
            pltpu.VMEM((8, POINTS), F32),
            pltpu.VMEM((CHUNKS, 16, PIECE), F32),
            pltpu.VMEM((BANDS, 8, 128), F32),
            pltpu.VMEM((BANDS, 8, 128), F32),
            pltpu.VMEM((16, 256), BF),
            pltpu.VMEM((MEMBERS, 16, 256), BF),
            pltpu.VMEM((ROWS * FIELDS, CHUNK), BF),
            pltpu.VMEM((ROWS * FIELDS, LON), F32),
            pltpu.VMEM((5, ROWS, LON), F32),
            pltpu.VMEM((16, STATIONS, FIELDS), F32),
            pltpu.VMEM((1, ROWS, FIELDS, LON), BF),
            pltpu.SemaphoreType.DMA((ROWS + 4,)),
            pltpu.SemaphoreType.DMA((2 + CHUNKS,)),
            sems, sems, sems, sems, sems, piece_sems, sems, sems, piece_sems,
        ],
        compiler_params=pltpu.CompilerParams(
            vmem_limit_bytes=56 * MIB, collective_id=0, has_side_effects=True
        ),
    )(
        block_band.reshape(-1), block_start, jnp.asarray(row_factors()), ensemble, mix_weight,
        station_weight.reshape(16, STATIONS * ROWS, 128),        station_obs, jnp.transpose(analysis, (1, 0, 2)), jnp.asarray(inverse_table()),
    )
    score, station, state = pl.pallas_call(
        hand_over,
        out_shape=shapes,
        in_specs=[vmem] * 3,
        out_specs=(vmem,) * 3,
        compiler_params=pltpu.CompilerParams(vmem_limit_bytes=16 * MIB),
    )(*outs)
    return jnp.transpose(score, (1, 0, 2)), station, state


def solution(mesh):
    return jax.shard_map(
        shards,
        mesh=mesh,
        in_specs=(
            P("member", "band", None, None),
            P(),
            P("band", "member", None),
            P("band", None, None, None),
            P("band", None, None),
            P(),
            P(),
        ),
        out_specs=(
            P("band", "member", None),
            P("band", None, None),
            P("member", "band", None, None),
        ),
        check_vma=False,
    )
```

time: 113 us -> 73.4 us (0.65)
  Pallas kernels: 96.8 us -> 72.6 us
  local copies, waits for them, and re-layouts: 11.8 us -> 0 us
  other arithmetic: 2.52 us -> 0 us
    pallas_call x1 -> x2, Pallas kernels: 96.8 us -> 72.6 us  [the longest x1 71.4 us: shards(): pl.pallas_call(kernel, out_shape=tuple((pltpu.VMEM(shape.shape, shape.dty...]
    unnamed x8 -> x0, local copies, waits for them, and re-layouts: 6.67 us -> none
    pallas_call x1 -> x0, local copies, waits for them, and re-layouts: 1.66 us -> none  [shards(): pl.pallas_call(kernel, out_shape=(jax.ShapeDtypeStruct((ROWS, 5, LON), F3...]
    unnamed x1 -> x0, other arithmetic: 1.34 us -> none
where the time goes in v2:
time: 73.4 us; the launch traced here: 73.2 us
  Pallas kernels  72.6 us (99%)
    pallas_call x1, Pallas kernels, shards(): pl.pallas_call(kernel, out_shape=tuple((pltpu.VMEM(shape.shape, shape.dty...  71.4 us

profile of v2, /device:TPU:1, one launch (start us, length us, event | category | flops | bytes accessed | tf_op | source)
XLA Modules:
  0.0 73.2 jit_solution(12327735042698388013)
XLA Ops:
  0.6 71.4 %shard_map.112 = (f32[5,4,1440]{2,1,0:T(4,128)S(1)}, f32[16,32,80]{2,1,0:T(8,128)S(1)}, bf16[1,4,80,1440]{3,2,1,0:T(8,128)(2,1)S(1)}) custom-call(s32[256]{0:T(256)} %bitcast.6, s32[256]{0:T(256)} %first_ref.1, f32[70,3]{1,0:T(8,128)} %constant.4.clone.factor_ref, bf16[1,4,80,1440]{3,2,1,0:T(8,128)(2,1)} %state_hbm.1, bf16[3,80,80]{2,1,0:T(8,128)(2,1)} %mix_ref.1, ...), custom_call_target="tpu_custom_call" | custom-call | tf_op jit(solution)/shard_map/pallas_call | solution.py:676
  72.0 1.2 %shard_map.113 = (f32[5,4,1440]{2,1,0:T(4,128)}, f32[16,32,80]{2,1,0:T(8,128)}, bf16[1,4,80,1440]{3,2,1,0:T(8,128)(2,1)}) custom-call(f32[5,4,1440]{2,1,0:T(4,128)S(1)} %get-tuple-element.9.refs_0_, f32[16,32,80]{2,1,0:T(8,128)S(1)} %get-tuple-element.10.refs_1_, bf16[1,4,80,1440]{3,2,1,0:T(8,128)(2,1)S(1)} %get-tuple-element.11.refs_2_), custom_call_target="tpu_custom_call" | custom-call | tf_op jit(solution)/shard_map/pallas_call | solution.py:732

commit v3 on v2

--- a/solution.py
+++ b/solution.py
@@ -162,12 +162,12 @@
     return score, grads
 
 
-def send(src, dst, sems, at, device):
+def send(src, dst, sems, device):
     return pltpu.make_async_remote_copy(
         src_ref=src,
         dst_ref=dst,
-        send_sem=sems.at[0, at],
-        recv_sem=sems.at[1, at],
+        send_sem=sems.at[0],
+        recv_sem=sems.at[1],
         device_id=device,
         device_id_type=pl.DeviceIdType.MESH,
     )
@@ -187,21 +187,20 @@
     @pl.loop(1, 16)
     def _(step):
         peer = at(me, step, 1)
-        send(source(peer), target(me), sems, step, {axis: peer}).start()
+        send(source(peer), target.at[me], sems, {axis: peer}).start()
+
+
+def all_others(target, sems, me, at, axis):
+    whole = target.at[0:15]
+    return send(whole, whole, sems, {axis: at(me, 1, 1)})
 
 
 def wait_received(source, target, sems, me, at, axis):
-    @pl.loop(1, 16)
-    def _(step):
-        peer = at(me, step, -1)
-        send(source(peer), target(peer), sems, step, {axis: peer}).wait_recv()
+    all_others(target, sems, me, at, axis).wait_recv()
 
 
 def wait_sent(source, target, sems, me, at, axis):
-    @pl.loop(1, 16)
-    def _(step):
-        peer = at(me, step, 1)
-        send(source(peer), target(me), sems, step, {axis: peer}).wait_send()
+    all_others(target, sems, me, at, axis).wait_send()
 
 
 def find_slots(band_ref, band, slot_ref):
@@ -503,36 +502,31 @@
     u[HALO : HALO + ROWS, :, :LON] = state_ref[0]
 
     def to_north(i):
-        return send(u.at[HALO + ROWS - 1 - i], u.at[HALO - 1 - i], halo_sem, i, {"band": band_at(band, 1, 1)})
+        return send(u.at[HALO + ROWS - 1 - i], u.at[HALO - 1 - i], halo_sem.at[i], {"band": band_at(band, 1, 1)})
 
     def to_south(i):
-        return send(u.at[HALO + i], u.at[HALO + ROWS + i], halo_sem, HALO + i, {"band": band_at(band, 1, -1)})
+        return send(u.at[HALO + i], u.at[HALO + ROWS + i], halo_sem.at[HALO + i], {"band": band_at(band, 1, -1)})
 
     def send_halo(i):
         pl.when(band < BANDS - 1)(to_north(i).start)
         pl.when(band > 0)(to_south(i).start)
 
-    direct_args = (lambda b: direct_out.at[b], lambda b: direct_in.at[b], direct_sem, band, band_at, "band")
-    weight_args = (lambda m: joined, lambda m: weights.at[m], weight_sem, member, member_at, "member")
-    z_args = (lambda b: zout.at[b], lambda b: zin.at[b], z_sem, band, band_at, "band")
-    obs_args = (lambda b: obs_out.at[b], lambda b: obs_in.at[b], obs_sem, band, band_at, "band")
-    station_args = (lambda b: station_out.at[b], lambda b: station_in.at[b], station_sem, band, band_at, "band")
-    own_args = (lambda m: own, lambda m: gathered.at[m], own_sem, member, member_at, "member")
+    direct_args = (lambda b: direct_out.at[b], direct_in, direct_sem, band, band_at, "band")
+    weight_args = (lambda m: joined, weights, weight_sem, member, member_at, "member")
+    z_args = (lambda b: zout.at[b], zin, z_sem, band, band_at, "band")
+    obs_args = (lambda b: obs_out.at[b], obs_in, obs_sem, band, band_at, "band")
+    station_args = (lambda b: station_out.at[b], station_in, station_sem, band, band_at, "band")
+    own_args = (lambda m: own, gathered, own_sem, member, member_at, "member")
 
     def message_args(q):
-        return (
-            lambda m: message.at[q, m], lambda m: received.at[q, m], message_sem.at[q], member, member_at, "member"
-        )
+        return lambda m: message.at[q, m], received.at[q], message_sem.at[q], member, member_at, "member"
 
     def grad_args(q):
-        return lambda m: grad.at[q, m], lambda m: returned.at[q, m], grad_sem.at[q], member, member_at, "member"
+        return lambda m: grad.at[q, m], returned.at[q], grad_sem.at[q], member, member_at, "member"
 
     def run_pair(layer, low, high):
         own = HALO <= low and high < HALO + ROWS
-
-        @pl.loop(0, 2)
-        def _(side):
-            row = low + side * (high - low)
+        for row in (low, high):
             factor = band * ROWS + row
             stencil_row(
                 layers.at[layer], layers.at[layer + 1], mix_ref[layer], row,
@@ -545,32 +539,32 @@
 
     run_pair(0, 4, 5)
     fetches[ROWS].wait()
+    outgoing_shares(slot_ref, weight_ref, member, zout)
+    fetches[ROWS + 1].wait()
+    outgoing_obs(slot_ref, obs_ref, member, obs_out)
+    outgoing_direct(slot_ref, weight_ref, turned, direct_out)
     pl.semaphore_wait(barrier, 30)
     send_halo(0)
-    outgoing_shares(slot_ref, weight_ref, member, zout)
     exchange(*z_args)
     send_halo(1)
     send_halo(2)
     zin[band] = zout[band]
-    fetches[ROWS + 1].wait()
-    outgoing_obs(slot_ref, obs_ref, member, obs_out)
     obs_in[band] = obs_out[band]
-    outgoing_direct(slot_ref, weight_ref, turned, direct_out)
     direct_in[band] = direct_out[band]
     find_starts(band_ref, first_ref, band, start_ref)
     fetches[ROWS + 2].wait()
     fold_truth(truth_ref, truth)
     wait_halo(0)
     run_pair(0, 3, 6)
+    run_pair(1, 4, 5)
     wait_received(*z_args)
     join_shares(zin, joined)
     exchange(*weight_args)
     weights[member] = joined[...]
-    run_pair(1, 4, 5)
     wait_halo(1)
+    run_pair(0, 2, 7)
     exchange(*obs_args)
     exchange(*direct_args)
-    run_pair(0, 2, 7)
     run_pair(1, 3, 6)
     run_pair(2, 4, 5)
     wait_halo(2)
@@ -590,8 +584,9 @@
     for q in range(CHUNKS - 1):
         wait_received(*message_args(q))
         station_rows(q, received, main, fifth, rows)
-        grid_pairs(q, received, values, truth, score)
         if q == 0:
+            grid_pairs(q, received, values, truth, score)
+        else:
             wait_received(*obs_args)
             join_obs(obs_in, obs)
             wait_received(*weight_args)
@@ -615,7 +610,7 @@
     back, back_fifth = message_to_station(True)
     for q in range(CHUNKS):
         spread_chunk(q, slopes, spread_weight, spread)
-        if q == CHUNKS - 1:
+        if q > 0:
             grid_pairs(q, received, values, truth, score)
         total_chunk(q, values, spread, back, back_fifth, grad)
         exchange(*grad_args(q))
@@ -666,8 +661,8 @@
     vmem = pl.BlockSpec(memory_space=pltpu.VMEM)
     anywhere = pl.BlockSpec(memory_space=pl.ANY)
     message = (CHUNKS, MEMBERS, 16, PIECE)
-    sems = pltpu.SemaphoreType.DMA((2, 16))
-    piece_sems = pltpu.SemaphoreType.DMA((CHUNKS, 2, 16))
+    sems = pltpu.SemaphoreType.DMA((2,))
+    piece_sems = pltpu.SemaphoreType.DMA((CHUNKS, 2))
     shapes = (
         jax.ShapeDtypeStruct((5, ROWS, LON), F32),
         jax.ShapeDtypeStruct((16, STATIONS, FIELDS), F32),
@@ -720,7 +715,8 @@
             pltpu.VMEM((1, ROWS, FIELDS, LON), BF),
             pltpu.SemaphoreType.DMA((ROWS + 4,)),
             pltpu.SemaphoreType.DMA((2 + CHUNKS,)),
-            sems, sems, sems, sems, sems, piece_sems, sems, sems, piece_sems,
+            pltpu.SemaphoreType.DMA((2 * HALO, 2)),
+            sems, sems, sems, sems, piece_sems, sems, sems, piece_sems,
         ],
         compiler_params=pltpu.CompilerParams(
             vmem_limit_bytes=56 * MIB, collective_id=0, has_side_effects=True

time: 73.4 us -> 66.4 us (0.905)
  Pallas kernels: 72.6 us -> 65.6 us
    pallas_call x1, Pallas kernels: 71.4 us -> 64.5 us  [shards(): pl.pallas_call(kernel, out_shape=tuple((pltpu.VMEM(shape.shape, shape.dty...]
where the time goes in v3:
time: 66.4 us; the launch traced here: 66.3 us
  Pallas kernels  65.6 us (99%)
    pallas_call x1, Pallas kernels, shards(): pl.pallas_call(kernel, out_shape=tuple((pltpu.VMEM(shape.shape, shape.dty...  64.5 us

profile of v3, /device:TPU:1, one launch (start us, length us, event | category | flops | bytes accessed | tf_op | source)
XLA Modules:
  0.0 66.3 jit_solution(2235547055370510530)
XLA Ops:
  0.6 64.5 %shard_map.112 = (f32[5,4,1440]{2,1,0:T(4,128)S(1)}, f32[16,32,80]{2,1,0:T(8,128)S(1)}, bf16[1,4,80,1440]{3,2,1,0:T(8,128)(2,1)S(1)}) custom-call(s32[256]{0:T(256)} %bitcast.6, s32[256]{0:T(256)} %first_ref.1, f32[70,3]{1,0:T(8,128)} %constant.4.clone.factor_ref, bf16[1,4,80,1440]{3,2,1,0:T(8,128)(2,1)} %state_hbm.1, bf16[3,80,80]{2,1,0:T(8,128)(2,1)} %mix_ref.1, ...), custom_call_target="tpu_custom_call" | custom-call | tf_op jit(solution)/shard_map/pallas_call | solution.py:671
  65.1 1.2 %shard_map.113 = (f32[5,4,1440]{2,1,0:T(4,128)}, f32[16,32,80]{2,1,0:T(8,128)}, bf16[1,4,80,1440]{3,2,1,0:T(8,128)(2,1)}) custom-call(f32[5,4,1440]{2,1,0:T(4,128)S(1)} %get-tuple-element.9.refs_0_, f32[16,32,80]{2,1,0:T(8,128)S(1)} %get-tuple-element.10.refs_1_, bf16[1,4,80,1440]{3,2,1,0:T(8,128)(2,1)S(1)} %get-tuple-element.11.refs_2_), custom_call_target="tpu_custom_call" | custom-call | tf_op jit(solution)/shard_map/pallas_call | solution.py:728

commit v4 on v3

--- a/solution.py
+++ b/solution.py
@@ -524,20 +524,27 @@
     def grad_args(q):
         return lambda m: grad.at[q, m], returned.at[q], grad_sem.at[q], member, member_at, "member"
 
-    def run_pair(layer, low, high):
-        own = HALO <= low and high < HALO + ROWS
-        for row in (low, high):
+    core = band & 1
+
+    def run(*steps):
+        for layer, place in steps:
+            row = place + core * (EXT - 1 - 2 * place)
             factor = band * ROWS + row
+            own = HALO <= place < HALO + ROWS
             stencil_row(
                 layers.at[layer], layers.at[layer + 1], mix_ref[layer], row,
                 factor_ref[factor, 0], factor_ref[factor, 1], None if own else factor_ref[factor, 2],
             )
 
-    def wait_halo(i):
-        pl.when(band > 0)(to_north(i).wait_recv)
-        pl.when(band < BANDS - 1)(to_south(i).wait_recv)
-
-    run_pair(0, 4, 5)
+    def wait_near(i):
+        pl.when(core == 1)(to_north(i).wait_recv)
+        pl.when(core == 0)(to_south(i).wait_recv)
+
+    def wait_far(i):
+        pl.when((core == 0) & (band > 0))(to_north(i).wait_recv)
+        pl.when((core == 1) & (band < BANDS - 1))(to_south(i).wait_recv)
+
+    run((0, 4), (0, 5))
     fetches[ROWS].wait()
     outgoing_shares(slot_ref, weight_ref, member, zout)
     fetches[ROWS + 1].wait()
@@ -554,23 +561,24 @@
     find_starts(band_ref, first_ref, band, start_ref)
     fetches[ROWS + 2].wait()
     fold_truth(truth_ref, truth)
-    wait_halo(0)
-    run_pair(0, 3, 6)
-    run_pair(1, 4, 5)
+    for i in range(HALO):
+        wait_near(i)
+    run((0, 6), (0, 7))
+    run((1, 5), (0, 8))
+    run((1, 6), (1, 7))
+    run((2, 6))
+    wait_far(0)
+    run((0, 3), (1, 4), (2, 5))
     wait_received(*z_args)
     join_shares(zin, joined)
     exchange(*weight_args)
     weights[member] = joined[...]
-    wait_halo(1)
-    run_pair(0, 2, 7)
+    wait_far(1)
+    run((0, 2), (1, 3), (2, 4))
+    wait_far(2)
     exchange(*obs_args)
     exchange(*direct_args)
-    run_pair(1, 3, 6)
-    run_pair(2, 4, 5)
-    wait_halo(2)
-    run_pair(0, 1, 8)
-    run_pair(1, 2, 7)
-    run_pair(2, 3, 6)
+    run((0, 1), (1, 2), (2, 3))
 
     fetches[ROWS + 3].wait()
     main, fifth = grid_to_message(False)
@@ -598,9 +606,6 @@
     station_rows(CHUNKS - 1, received, main, fifth, rows)
     estimates(CHUNK * (CHUNKS - 1), LANES, rows, spread_weight, est)
     station_scores(est, slopes, obs, station_out)
-    exchange(*station_args)
-    station_in[band] = station_out[band]
-
     def share_station_scores():
         wait_received(*station_args)
         own_station_scores(slot_ref, station_in, own)
@@ -614,6 +619,9 @@
             grid_pairs(q, received, values, truth, score)
         total_chunk(q, values, spread, back, back_fifth, grad)
         exchange(*grad_args(q))
+        if q == 0:
+            exchange(*station_args)
+            station_in[band] = station_out[band]
         returned[q, member] = grad[q, member]
 
     leave = [

time: 66.4 us -> 68.6 us (1.033)
  Pallas kernels: 65.6 us -> 67.8 us
    pallas_call x1, Pallas kernels: 64.5 us -> 66.6 us  [shards(): pl.pallas_call(kernel, out_shape=tuple((pltpu.VMEM(shape.shape, shape.dty...]
where the time goes in v4:
time: 68.6 us; the launch traced here: 68.4 us
  Pallas kernels  67.8 us (99%)
    pallas_call x1, Pallas kernels, shards(): pl.pallas_call(kernel, out_shape=tuple((pltpu.VMEM(shape.shape, shape.dty...  66.6 us

profile of v4, /device:TPU:1, one launch (start us, length us, event | category | flops | bytes accessed | tf_op | source)
XLA Modules:
  0.0 68.4 jit_solution(9019975758694864268)
XLA Ops:
  0.6 66.6 %shard_map.112 = (f32[5,4,1440]{2,1,0:T(4,128)S(1)}, f32[16,32,80]{2,1,0:T(8,128)S(1)}, bf16[1,4,80,1440]{3,2,1,0:T(8,128)(2,1)S(1)}) custom-call(s32[256]{0:T(256)} %bitcast.6, s32[256]{0:T(256)} %first_ref.1, f32[70,3]{1,0:T(8,128)} %constant.4.clone.factor_ref, bf16[1,4,80,1440]{3,2,1,0:T(8,128)(2,1)} %state_hbm.1, bf16[3,80,80]{2,1,0:T(8,128)(2,1)} %mix_ref.1, ...), custom_call_target="tpu_custom_call" | custom-call | tf_op jit(solution)/shard_map/pallas_call | solution.py:679
  67.3 1.2 %shard_map.113 = (f32[5,4,1440]{2,1,0:T(4,128)}, f32[16,32,80]{2,1,0:T(8,128)}, bf16[1,4,80,1440]{3,2,1,0:T(8,128)(2,1)}) custom-call(f32[5,4,1440]{2,1,0:T(4,128)S(1)} %get-tuple-element.9.refs_0_, f32[16,32,80]{2,1,0:T(8,128)S(1)} %get-tuple-element.10.refs_1_, bf16[1,4,80,1440]{3,2,1,0:T(8,128)(2,1)S(1)} %get-tuple-element.11.refs_2_), custom_call_target="tpu_custom_call" | custom-call | tf_op jit(solution)/shard_map/pallas_call | solution.py:736

commit v5 on v3

--- a/solution.py
+++ b/solution.py
@@ -584,9 +584,8 @@
     for q in range(CHUNKS - 1):
         wait_received(*message_args(q))
         station_rows(q, received, main, fifth, rows)
-        if q == 0:
-            grid_pairs(q, received, values, truth, score)
-        else:
+        grid_pairs(q, received, values, truth, score)
+        if q == CHUNKS - 2:
             wait_received(*obs_args)
             join_obs(obs_in, obs)
             wait_received(*weight_args)
@@ -598,9 +597,6 @@
     station_rows(CHUNKS - 1, received, main, fifth, rows)
     estimates(CHUNK * (CHUNKS - 1), LANES, rows, spread_weight, est)
     station_scores(est, slopes, obs, station_out)
-    exchange(*station_args)
-    station_in[band] = station_out[band]
-
     def share_station_scores():
         wait_received(*station_args)
         own_station_scores(slot_ref, station_in, own)
@@ -610,10 +606,13 @@
     back, back_fifth = message_to_station(True)
     for q in range(CHUNKS):
         spread_chunk(q, slopes, spread_weight, spread)
-        if q > 0:
+        if q == CHUNKS - 1:
             grid_pairs(q, received, values, truth, score)
         total_chunk(q, values, spread, back, back_fifth, grad)
         exchange(*grad_args(q))
+        if q == 0:
+            exchange(*station_args)
+            station_in[band] = station_out[band]
         returned[q, member] = grad[q, member]
 
     leave = [

time: 66.4 us -> 66.8 us (level)
  no operation moved by 1% of the time
where the time goes in v5:
time: 66.8 us; the launch traced here: 66.7 us
  Pallas kernels  66 us (99%)
    pallas_call x1, Pallas kernels, shards(): pl.pallas_call(kernel, out_shape=tuple((pltpu.VMEM(shape.shape, shape.dty...  64.9 us

profile of v5, /device:TPU:1, one launch (start us, length us, event | category | flops | bytes accessed | tf_op | source)
XLA Modules:
  0.0 66.7 jit_solution(10348468576922191117)
XLA Ops:
  0.6 64.9 %shard_map.112 = (f32[5,4,1440]{2,1,0:T(4,128)S(1)}, f32[16,32,80]{2,1,0:T(8,128)S(1)}, bf16[1,4,80,1440]{3,2,1,0:T(8,128)(2,1)S(1)}) custom-call(s32[256]{0:T(256)} %bitcast.6, s32[256]{0:T(256)} %first_ref.1, f32[70,3]{1,0:T(8,128)} %constant.4.clone.factor_ref, bf16[1,4,80,1440]{3,2,1,0:T(8,128)(2,1)} %state_hbm.1, bf16[3,80,80]{2,1,0:T(8,128)(2,1)} %mix_ref.1, ...), custom_call_target="tpu_custom_call" | custom-call | tf_op jit(solution)/shard_map/pallas_call | solution.py:670
  65.5 1.2 %shard_map.113 = (f32[5,4,1440]{2,1,0:T(4,128)}, f32[16,32,80]{2,1,0:T(8,128)}, bf16[1,4,80,1440]{3,2,1,0:T(8,128)(2,1)}) custom-call(f32[5,4,1440]{2,1,0:T(4,128)S(1)} %get-tuple-element.9.refs_0_, f32[16,32,80]{2,1,0:T(8,128)S(1)} %get-tuple-element.10.refs_1_, bf16[1,4,80,1440]{3,2,1,0:T(8,128)(2,1)S(1)} %get-tuple-element.11.refs_2_), custom_call_target="tpu_custom_call" | custom-call | tf_op jit(solution)/shard_map/pallas_call | solution.py:727
